TPU v7x, 32 devices: a whole 2x2x4 slice. The times are simulated.
32 devices in a mesh: lat: 8 (over z, x), depth: 4 (over y, core).
Axes of the slice: x: 2, y: 2, z: 4, core: 2. Of those that a mesh axis runs over, the one named last changes fastest.
Arguments:
- head: float32 [64, 64, 4096], P('depth', 'lat'), may hold values from -1 to 0.5
- head_old: float32 [64, 64, 4096], P('depth', 'lat'), may hold values from -1 to 0.5
- soil: int32 [64, 64, 4096], P('depth', 'lat'), may hold values from 0 to 11
- cond_table: float32 [12], replicated, may hold values from 0.3 to 2
- shape_table: float32 [12], replicated, may hold values from 0.3 to 1.5
- pore_table: float32 [12], replicated, may hold values from 0.2 to 0.5
- pond: float32 [64, 4096], P('lat'), may hold values from 0.02 to 0.6
- ground: float32 [64, 4096], P('lat'), may hold values from -1.5 to 1.5
- ponded: int32 [64, 4096], P('lat'), may hold values 0 or 1
- river: int32 [64, 4096], P('lat'), may hold values 0 or 1
Outputs:
- head_new: float32 [64, 64, 4096], P('depth', 'lat')
- surface_new: float32 [64, 4096], P('lat', 'depth')
All inputs are finite; a program needn't handle non-finite values. No bound on the sum of `ponded` or of `river` on one device may be relied on, other than what follows from the above.
Results may differ from a plain program's by a relative error of at most 0.0003.
Values sent between devices are 32-bit elements; how exact they have to be, the bound alone decides.
A program may use at most 128 MiB of HBM per device.

v0:
```python
import jax
import jax.numpy as jnp
from jax import lax
from jax.sharding import PartitionSpec as P

SWEEPS = 4


TIME_STEP = 20.0
SURFACE_STEP = 2.0
SPECIFIC_STORAGE = 0.01
LAND_CONVEYANCE = 3.0
RIVER_CONVEYANCE = 10.0
SLOPE_FLOOR = 0.01


def with_halo(x, sides, width):
    for axis, dim in sides:
        size, length = (lax.axis_size(axis), x.shape[dim])
        up = [(i, (i + 1) % size) for i in range(size - 1)]
        down = [(j, i) for i, j in up]
        last = lax.slice_in_dim(x, length - width, length, axis=dim)
        initial = lax.slice_in_dim(x, 0, width, axis=dim)
        before = lax.ppermute(last, axis, up)
        after = lax.ppermute(initial, axis, down)
        x = jnp.concatenate([before, x, after], axis=dim)
    return x


def from_root(value, axis, source):
    kept = jnp.where(lax.axis_index(axis) == source, value, 0).astype(value.dtype)
    return lax.psum(kept, axis)


def lookup(soil, table):
    value = jnp.zeros(soil.shape, jnp.float32)
    for soil_kind in range(table.shape[0]):
        value = jnp.where(soil == soil_kind, table[soil_kind], value)
    return value


def harmonic(first, second):
    total = first + second
    return 2.0 * first * second / jnp.where(total > 0.0, total, 1.0)


def soil_state(head, head_old, soil, cond_table, shape_table, pore_table):
    saturated = lookup(soil, cond_table)
    steepness = lookup(soil, shape_table)
    porosity = lookup(soil, pore_table)
    wetness = jnp.exp(steepness * jnp.minimum(head, 0.0))
    wetness_old = jnp.exp(steepness * jnp.minimum(head_old, 0.0))
    conductivity = saturated * wetness
    storage_change = porosity * (wetness - wetness_old) + SPECIFIC_STORAGE * (head - head_old)
    capacity = SPECIFIC_STORAGE + porosity * steepness * wetness
    return (conductivity, storage_change, capacity)


def vertical_terms(cond_ext, head_ext):
    vface = harmonic(cond_ext[:-1], cond_ext[1:])
    vflux = vface * (head_ext[:-1] - head_ext[1:] + 1.0)
    return (vface, vflux)


def lateral_inflow(conductivity, head, cond_rows, head_rows):
    face_x = harmonic(cond_rows[:, :-1], cond_rows[:, 1:])
    inflow = face_x[:, 1:] * (head_rows[:, 2:] - head) + face_x[:, :-1] * (head_rows[:, :-2] - head)
    cond_cols = jnp.pad(conductivity, ((0, 0), (0, 0), (1, 1)))
    head_cols = jnp.pad(head, ((0, 0), (0, 0), (1, 1)))
    face_y = harmonic(cond_cols[:, :, :-1], cond_cols[:, :, 1:])
    inflow = inflow + face_y[:, :, 1:] * (head_cols[:, :, 2:] - head)
    return inflow + face_y[:, :, :-1] * (head_cols[:, :, :-2] - head)


def newton_system(storage_change, capacity, vface, vflux, lateral, top_term, top_cond, bottom_term):
    inflow = jnp.concatenate([(vflux[0] + top_term)[None], vflux[1:-1]], 0)
    outflow = jnp.concatenate([vflux[1:-1], (vflux[-1] + bottom_term)[None]], 0)
    residual = storage_change / TIME_STEP - (inflow - outflow) - lateral
    diagonal = capacity / TIME_STEP + vface[:-1] + vface[1:]
    diagonal = jnp.concatenate([(diagonal[0] + 2.0 * top_cond)[None], diagonal[1:]], 0)
    return (residual, diagonal, -vface[:-1], -vface[1:])


def thomas(lower, middle, upper, rhs):
    count = middle.shape[0]
    ratios = []
    partial_values = []
    for row_index in range(count):
        if row_index == 0:
            pivot = middle[0]
            partial_values.append(rhs[0] / pivot)
        else:
            pivot = middle[row_index] - lower[row_index] * ratios[-1]
            partial_values.append((rhs[row_index] - lower[row_index] * partial_values[-1]) / pivot)
        ratios.append(upper[row_index] / pivot)
    result = [partial_values[-1]]
    for row_index in reversed(range(count - 1)):
        result.insert(0, partial_values[row_index] - ratios[row_index] * result[0])
    return jnp.stack(result, 0)


def reduced_down(pieces, beta_prev, gamma_prev):
    top_base, bottom_base, top_above, bottom_above, top_below, bottom_below = pieces
    scale = 1.0 - top_above * gamma_prev
    tau_value = (top_base - top_above * beta_prev) / scale
    sigma_value = top_below / scale
    beta_value = bottom_base - bottom_above * beta_prev + bottom_above * gamma_prev * tau_value
    gamma_value = bottom_below + bottom_above * gamma_prev * sigma_value
    return (beta_value, gamma_value, tau_value, sigma_value)


def face_k(pond_one, ground_one, conv_one, pond_two, ground_two, conv_two):
    depth_face = 0.5 * (pond_one + pond_two)
    slope = pond_two + ground_two - (pond_one + ground_one)
    return (
        jnp.power(depth_face, 5.0 / 3.0)
        * harmonic(conv_one, conv_two)
        / jnp.sqrt(jnp.abs(slope) + SLOPE_FLOOR)
    )


def row_terms(
    pond, ground, conv, exfil, pond_up, ground_up, conv_up, pond_down, ground_down, conv_down
):
    k_up = face_k(pond, ground, conv, pond_up, ground_up, conv_up)
    k_down = face_k(pond, ground, conv, pond_down, ground_down, conv_down)
    k_cols = face_k(
        pond[:, :-1], ground[:, :-1], conv[:, :-1], pond[:, 1:], ground[:, 1:], conv[:, 1:]
    )
    k_left = jnp.pad(k_cols, ((0, 0), (1, 0)))
    k_right = jnp.pad(k_cols, ((0, 0), (0, 1)))
    ground_left = jnp.pad(ground[:, :-1], ((0, 0), (1, 0)))
    ground_right = jnp.pad(ground[:, 1:], ((0, 0), (0, 1)))
    sdiag = 1.0 / SURFACE_STEP + k_up + k_down + k_left + k_right
    srhs = (
        pond / SURFACE_STEP + exfil + k_up * (ground_up - ground) + k_down * (ground_down - ground)
    )
    srhs = srhs + k_left * (ground_left - ground) + k_right * (ground_right - ground)
    return (k_up, k_down, k_left, k_right, sdiag, srhs)


def sweep(level, level_up, level_down, terms):
    k_up, k_down, k_left, k_right, sdiag, srhs = terms
    left = jnp.pad(level[:, :-1], ((0, 0), (1, 0)))
    right = jnp.pad(level[:, 1:], ((0, 0), (0, 1)))
    return (srhs + k_up * level_up + k_down * level_down + k_left * left + k_right * right) / sdiag


def per_device(
    head, head_old, soil, cond_table, shape_table, pore_table, pond, ground, ponded, river
):
    depth_index = lax.axis_index("depth")
    depth_count = lax.axis_size("depth")
    is_top = depth_index == 0
    is_bottom = depth_index == depth_count - 1
    conductivity, storage_change, capacity = soil_state(
        head, head_old, soil, cond_table, shape_table, pore_table
    )
    head_ext, cond_ext = (
        with_halo(head, (("lat", 1), ("depth", 0)), 1),
        with_halo(conductivity, (("lat", 1), ("depth", 0)), 1),
    )
    vface, vflux = vertical_terms(cond_ext[:, 1:-1], head_ext[:, 1:-1])
    lateral = lateral_inflow(conductivity, head, cond_ext[1:-1], head_ext[1:-1])
    wet_pond = ponded.astype(jnp.float32) * pond
    top_flux = conductivity[0] * (2.0 * (wet_pond - head[0]) + 1.0)
    exfil = from_root(-top_flux, "depth", 0)
    zero_plane = jnp.zeros_like(top_flux)
    top_term = jnp.where(is_top, top_flux, zero_plane)
    top_cond = jnp.where(is_top, conductivity[0], zero_plane)
    bottom_term = jnp.where(is_bottom, conductivity[-1], zero_plane)
    residual, diagonal, lower, upper = newton_system(
        storage_change, capacity, vface, vflux, lateral, top_term, top_cond, bottom_term
    )
    local_lower = jnp.concatenate([zero_plane[None], lower[1:]], 0)
    local_upper = jnp.concatenate([upper[:-1], zero_plane[None]], 0)
    coupling_up = jnp.concatenate([lower[:1], jnp.zeros_like(lower[1:])], 0)
    coupling_down = jnp.concatenate([jnp.zeros_like(upper[:-1]), upper[-1:]], 0)
    stacked_rhs = jnp.stack([-residual, coupling_up, coupling_down], axis=1)
    solved = thomas(local_lower, diagonal, local_upper, stacked_rhs)
    base_part = solved[:, 0]
    above_part = solved[:, 1]
    below_part = solved[:, 2]
    pieces = (
        base_part[0],
        base_part[-1],
        above_part[0],
        above_part[-1],
        below_part[0],
        below_part[-1],
    )
    gathered = (
        lax.all_gather(pieces[0][None], "depth", axis=0, tiled=True),
        lax.all_gather(pieces[1][None], "depth", axis=0, tiled=True),
        lax.all_gather(pieces[2][None], "depth", axis=0, tiled=True),
        lax.all_gather(pieces[3][None], "depth", axis=0, tiled=True),
        lax.all_gather(pieces[4][None], "depth", axis=0, tiled=True),
        lax.all_gather(pieces[5][None], "depth", axis=0, tiled=True),
    )
    beta_prev = zero_plane
    gamma_prev = zero_plane
    downward = []
    for slab_index in range(depth_count):
        slab_pieces = tuple((member[slab_index] for member in gathered))
        result = reduced_down(slab_pieces, beta_prev, gamma_prev)
        downward.append((beta_prev, gamma_prev) + result)
        beta_prev = result[0]
        gamma_prev = result[1]
    tops_list = [zero_plane] * depth_count
    belows_list = [zero_plane] * depth_count
    carried = zero_plane
    for slab_index in reversed(range(depth_count)):
        belows_list[slab_index] = carried
        tops_list[slab_index] = downward[slab_index][4] - downward[slab_index][5] * carried
        carried = tops_list[slab_index]
    aboves_list = [
        downward[slab_index][0] - downward[slab_index][1] * tops_list[slab_index]
        for slab_index in range(depth_count)
    ]
    above_bottom = lax.dynamic_index_in_dim(
        jnp.stack(aboves_list, 0), depth_index, 0, keepdims=False
    )
    below_top = lax.dynamic_index_in_dim(jnp.stack(belows_list, 0), depth_index, 0, keepdims=False)
    step = base_part - above_part * above_bottom - below_part * below_top
    head_new = head + step
    conveyance = LAND_CONVEYANCE + (RIVER_CONVEYANCE - LAND_CONVEYANCE) * river.astype(jnp.float32)
    pond_ext, ground_ext, conv_ext = (
        with_halo(pond, (("lat", 0),), 1),
        with_halo(ground, (("lat", 0),), 1),
        with_halo(conveyance, (("lat", 0),), 1),
    )
    terms = row_terms(
        pond,
        ground,
        conveyance,
        exfil,
        pond_ext[:-2],
        ground_ext[:-2],
        conv_ext[:-2],
        pond_ext[2:],
        ground_ext[2:],
        conv_ext[2:],
    )
    level = pond
    for sweep_index in range(SWEEPS):
        level_ext = with_halo(level, (("lat", 0),), 1)
        level = sweep(level, level_ext[:-2], level_ext[2:], terms)
    column_width = pond.shape[1] // depth_count
    surface_new = lax.dynamic_slice_in_dim(level, depth_index * column_width, column_width, 1)
    return (head_new, surface_new)


def solution(mesh):
    placed = (
        P("depth", "lat", None),
        P("depth", "lat", None),
        P("depth", "lat", None),
        P(),
        P(),
        P(),
        P("lat", None),
        P("lat", None),
        P("lat", None),
        P("lat", None),
    )
    return jax.shard_map(
        per_device,
        mesh=mesh,
        in_specs=placed,
        out_specs=(P("depth", "lat", None), P("lat", "depth")),
        check_vma=False,
    )
```

profile of v0, /device:TPU:13, one launch (start us, length us, event | category | flops | bytes accessed | tf_op | source)
XLA Modules:
  0.0 227.2 jit_solution(15280895173623719091)
XLA Ops:
  10.9 23.3 %select_multiply_fusion = (f32[16,8,4096]{2,1,0:T(8,128)S(1)}, pred[16,8,4096]{2,1,0:T(8,128)(4,1)S(1)}, pred[16,8,4096]{2,1,0:T(8,128)(4,1)S(1)}, pred[16,8,409...) fusion(f32[16,8,4096]{2,1,0:T(8,128)} %param.10, ...), kind=kLoop, calls=%fused_computation.53 | loop fusion | flops 20447232 | bytes 12583008 | tf_op jit(solution)/shard_map/mul | solution.py:53
  37.0 3.1 %collective-permute-start.12 = (f32[1,4096]{1,0:T(1,128)S(1)}, f32[1,4096]{1,0:T(1,128)S(1)}, u32[]{:S(2)}, u32[]{:S(2)}) collective-permute-start(f32[1,4096]{1,0:T(1,128)S(1)} %get-tuple-element.137), channel_id=1, source_target_pairs={{4,0},{8,4},{12,8},{16,12},{20,16},{24,20},{28,24},{5,1},{9,5},{13... | collective-permute-start | bytes 49160 | tf_op jit(solution)/shard_map/ppermute | solution.py:25
  43.0 4.0 %collective-permute-start.10 = (f32[1,4096]{1,0:T(1,128)}, f32[1,4096]{1,0:T(1,128)S(1)}, u32[]{:S(2)}, u32[]{:S(2)}) collective-permute-start(f32[1,4096]{1,0:T(1,128)} %get-tuple-element.140), channel_id=1, source_target_pairs={{0,4},{4,8},{8,12},{12,16},{16,20},{20,24},{24,28},{1,5},{5,9},{9,... | collective-permute-start | bytes 49160 | tf_op jit(solution)/shard_map/ppermute | solution.py:24
  49.8 3.0 %collective-permute-start.13 = (f32[1,4096]{1,0:T(1,128)}, f32[1,4096]{1,0:T(1,128)}, u32[]{:S(2)}, u32[]{:S(2)}) collective-permute-start(f32[1,4096]{1,0:T(1,128)} %get-tuple-element.139), channel_id=1, source_target_pairs={{4,0},{8,4},{12,8},{16,12},{20,16},{24,20},{28,24},{5,1},{9,5},{13... | collective-permute-start | bytes 49160 | tf_op jit(solution)/shard_map/ppermute | solution.py:25
  53.8 3.5 %fusion.190 = (f32[16,1,4096]{2,1,0:T(1,128)}, f32[16,1,4096]{2,1,0:T(1,128)}) fusion(f32[16,8,4096]{2,1,0:T(8,128)} %copy-done.1), kind=kLoop, calls=%fused_computation.374 | loop fusion | bytes 1048576 | tf_op jit(solution)/shard_map/slice | solution.py:22
  64.1 4.0 %collective-permute-start = (f32[16,1,4096]{2,1,0:T(1,128)}, f32[16,1,4096]{2,1,0:T(1,128)}, u32[]{:S(2)}, u32[]{:S(2)}) collective-permute-start(f32[16,1,4096]{2,1,0:T(1,128)} %get-tuple-element.108), channel_id=1, source_target_pairs={{0,4},{4,8},{8,12},{12,16},{16,20},{20,24},{24,28},{1,5},{5,9},{9,... | collective-permute-start | bytes 786440 | tf_op jit(solution)/shard_map/ppermute | solution.py:24
  70.3 3.1 %collective-permute-start.4 = (f32[16,1,4096]{2,1,0:T(1,128)}, f32[16,1,4096]{2,1,0:T(1,128)}, u32[]{:S(2)}, u32[]{:S(2)}) collective-permute-start(f32[16,1,4096]{2,1,0:T(1,128)} %get-tuple-element.110), channel_id=1, source_target_pairs={{0,4},{4,8},{8,12},{12,16},{16,20},{20,24},{24,28},{1,5},{5,9},{9,... | collective-permute-start | bytes 786440 | tf_op jit(solution)/shard_map/ppermute | solution.py:24
  78.1 3.3 %collective-permute-start.14 = (f32[1,4096]{1,0:T(1,128)S(1)}, f32[1,4096]{1,0:T(1,128)S(1)}, u32[]{:S(2)}, u32[]{:S(2)}) collective-permute-start(f32[1,4096]{1,0:T(1,128)S(1)} %get-tuple-element.128), channel_id=1, source_target_pairs={{0,4},{4,8},{8,12},{12,16},{16,20},{20,24},{24,28},{1,5},{5,9},{9,... | collective-permute-start | bytes 49160 | tf_op jit(solution)/shard_map/ppermute | solution.py:24
  81.4 3.0 %collective-permute-start.15 = (f32[1,4096]{1,0:T(1,128)S(1)}, f32[1,4096]{1,0:T(1,128)S(1)}, u32[]{:S(2)}, u32[]{:S(2)}) collective-permute-start(f32[1,4096]{1,0:T(1,128)S(1)} %get-tuple-element.129), channel_id=1, source_target_pairs={{4,0},{8,4},{12,8},{16,12},{20,16},{24,20},{28,24},{5,1},{9,5},{13... | collective-permute-start | bytes 49160 | tf_op jit(solution)/shard_map/ppermute | solution.py:25
  86.8 3.4 %collective-permute-start.16 = (f32[1,4096]{1,0:T(1,128)S(1)}, f32[1,4096]{1,0:T(1,128)S(1)}, u32[]{:S(2)}, u32[]{:S(2)}) collective-permute-start(f32[1,4096]{1,0:T(1,128)S(1)} %get-tuple-element.124), channel_id=1, source_target_pairs={{0,4},{4,8},{8,12},{12,16},{16,20},{20,24},{24,28},{1,5},{5,9},{9,... | collective-permute-start | bytes 49160 | tf_op jit(solution)/shard_map/ppermute | solution.py:24
  90.2 2.8 %collective-permute-start.17 = (f32[1,4096]{1,0:T(1,128)S(1)}, f32[1,4096]{1,0:T(1,128)S(1)}, u32[]{:S(2)}, u32[]{:S(2)}) collective-permute-start(f32[1,4096]{1,0:T(1,128)S(1)} %get-tuple-element.125), channel_id=1, source_target_pairs={{4,0},{8,4},{12,8},{16,12},{20,16},{24,20},{28,24},{5,1},{9,5},{13... | collective-permute-start | bytes 49160 | tf_op jit(solution)/shard_map/ppermute | solution.py:25
  94.9 4.3 %collective-permute-start.18 = (f32[1,4096]{1,0:T(1,128)S(1)}, f32[1,4096]{1,0:T(1,128)S(1)}, u32[]{:S(2)}, u32[]{:S(2)}) collective-permute-start(f32[1,4096]{1,0:T(1,128)S(1)} %get-tuple-element.119), channel_id=1, source_target_pairs={{0,4},{4,8},{8,12},{12,16},{16,20},{20,24},{24,28},{1,5},{5,9},{9,... | collective-permute-start | bytes 49160 | tf_op jit(solution)/shard_map/ppermute | solution.py:24
  101.2 2.8 %collective-permute-start.5 = (f32[16,1,4096]{2,1,0:T(1,128)S(1)}, f32[16,1,4096]{2,1,0:T(1,128)S(1)}, u32[]{:S(2)}, u32[]{:S(2)}) collective-permute-start(f32[16,1,4096]{2,1,0:T(1,128)S(1)} %copy-done.21), channel_id=1, source_target_pairs={{4,0},{8,4},{12,8},{16,12},{20,16},{24,20},{28,24},{5,1},{9,5},{13... | collective-permute-start | bytes 786440 | tf_op jit(solution)/shard_map/ppermute | solution.py:25
  107.7 9.2 %collective-permute-start.3 = (f32[1,10,4096]{2,1,0:T(8,128)S(1)}, f32[1,10,4096]{2,1,0:T(8,128)S(1)}, u32[]{:S(2)}, u32[]{:S(2)}) collective-permute-start(f32[1,10,4096]{2,1,0:T(8,128)S(1)} %get-tuple-element.78), channel_id=1, source_target_pairs={{1,0},{2,1},{3,2},{5,4},{6,5},{7,6},{9,8},{10,9},{11,10},{13,12},{... | collective-permute-start | bytes 491528 | tf_op jit(solution)/shard_map/ppermute | solution.py:25
  119.0 4.5 %collective-permute-start.7 = (f32[1,10,4096]{2,1,0:T(8,128)S(1)}, f32[1,10,4096]{2,1,0:T(8,128)S(1)}, u32[]{:S(2)}, u32[]{:S(2)}) collective-permute-start(f32[1,10,4096]{2,1,0:T(8,128)S(1)} %get-tuple-element.80), channel_id=1, source_target_pairs={{1,0},{2,1},{3,2},{5,4},{6,5},{7,6},{9,8},{10,9},{11,10},{13,12},{... | collective-permute-start | bytes 491528 | tf_op jit(solution)/shard_map/ppermute | solution.py:25
  126.1 3.8 %fusion.7 = (f32[17,8,4096]{2,1,0:T(8,128)S(1)}, f32[17,8,4096]{2,1,0:T(8,128)S(1)}) fusion(f32[1,10,4096]{2,1,0:T(8,128)S(1)} %collective-permute-done.7, f32[16,1,4096]{2,1,0:T(1,128)S(1)} %collective-permute-done.5, f32[16,8,4096]{2,1,0:T(8,128)S(1)} %copy-done, f32[16,1,4096]{2,1,0:T(1,128)} %collective-permute-done.4, ...), kind=kLoop, calls=%fused_computation.13 | loop fusion | flops 11698176 | bytes 10354688 | tf_op jit(solution)/shard_map/mul | solution.py:61
  132.2 23.2 %fusion.17 = (f32[16,1,8,4096]{3,2,1,0:T(8,128)S(1)}, f32[16,8,4096]{2,1,0:T(8,128)S(1)}) fusion(f32[16,8,4097]{2,1,0:T(8,128)S(1)} %copy-done.4, f32[16,8,4096]{2,1,0:T(8,128)S(1)} %copy-done, f32[16,1,4096]{2,1,0:T(1,128)} %collective-permute-done.4, f32[16,9,4096]{2,1,0:T(8,128)S(1)} %fusion, f32[16,1,4096]{2,1,0:T(1,128)S(1)} %collective-permute-done.5, ...), kind=kLoop, calls=%fused_computation.38 | loop fusion | flops 27787264 | bytes 25821280 | tf_op jit(solution)/shard_map/stack | solution.py:179
  155.4 10.9 %add_add_fusion = f32[16,8,4096]{2,1,0:T(8,128)S(1)} fusion(f32[16,8,4096]{2,1,0:T(8,128)S(1)} %get-tuple-element.60, f32[16,8,4096]{2,1,0:T(8,128)S(1)} %copy-done, f32[17,8,4096]{2,1,0:T(8,128)S(1)} %get-tuple-element.62, pred[16,8,4096]{2,1,0:T(8,128)(4,1)S(1)} %copy-done.14, pred[16,8,4096]{2,1,0:T(8,128)(4,1)S(1)} %copy-done.13, ...), kind=kLoop, calls=%fused_computation.50 | loop fusion | flops 10485760 | bytes 16777264 | tf_op jit(solution)/shard_map/add | solution.py:79
  170.3 10.2 %all-gather = f32[4,1,8,4096]{3,2,1,0:T(8,128)S(1)} all-gather(f32[1,1,8,4096]{3,2,1,0:T(8,128)S(1)} %get-tuple-element.117), channel_id=2, replica_groups=mesh['lat'=8,'depth'=4] {'depth'}, dimensions={0}, use_global_device_ids=true | all-gather | bytes 655360 | tf_op jit(solution)/shard_map/all_gather | solution.py:193
  180.5 7.3 %all-gather.1 = f32[4,1,8,4096]{3,2,1,0:T(8,128)S(1)} all-gather(f32[1,1,8,4096]{3,2,1,0:T(8,128)S(1)} %get-tuple-element.116), channel_id=3, replica_groups=mesh['lat'=8,'depth'=4] {'depth'}, dimensions={0}, use_global_device_ids=true | all-gather | bytes 655360 | tf_op jit(solution)/shard_map/all_gather | solution.py:195
  187.8 7.3 %all-gather.2 = f32[4,1,8,4096]{3,2,1,0:T(8,128)S(1)} all-gather(f32[1,1,8,4096]{3,2,1,0:T(8,128)S(1)} %get-tuple-element.115), channel_id=4, replica_groups=mesh['lat'=8,'depth'=4] {'depth'}, dimensions={0}, use_global_device_ids=true | all-gather | bytes 655360 | tf_op jit(solution)/shard_map/all_gather | solution.py:197
  195.1 7.3 %all-gather.3 = f32[4,1,8,4096]{3,2,1,0:T(8,128)S(1)} all-gather(f32[1,1,8,4096]{3,2,1,0:T(8,128)S(1)} %get-tuple-element.114), channel_id=5, replica_groups=mesh['lat'=8,'depth'=4] {'depth'}, dimensions={0}, use_global_device_ids=true | all-gather | bytes 655360 | tf_op jit(solution)/shard_map/all_gather | solution.py:194
  202.4 7.3 %all-gather.4 = f32[4,1,8,4096]{3,2,1,0:T(8,128)S(1)} all-gather(f32[1,1,8,4096]{3,2,1,0:T(8,128)S(1)} %get-tuple-element.113), channel_id=6, replica_groups=mesh['lat'=8,'depth'=4] {'depth'}, dimensions={0}, use_global_device_ids=true | all-gather | bytes 655360 | tf_op jit(solution)/shard_map/all_gather | solution.py:196
  209.7 7.3 %all-gather.5 = f32[4,1,8,4096]{3,2,1,0:T(8,128)S(1)} all-gather(f32[1,1,8,4096]{3,2,1,0:T(8,128)S(1)} %get-tuple-element.112), channel_id=7, replica_groups=mesh['lat'=8,'depth'=4] {'depth'}, dimensions={0}, use_global_device_ids=true | all-gather | bytes 655360 | tf_op jit(solution)/shard_map/all_gather | solution.py:198
  (151 shorter events, 50.6 us)
Async XLA Ops:
  7.2 69.3 %all-reduce.17.cloned.1.call-start = ((), (), s32[]{:S(2)}) async-start(), calls=%async_computation | async-start | bytes 262144 | tf_op jit(solution)/shard_map/psum | solution.py:32
  10.8 24.7 %copy-start = (f32[16,8,4096]{2,1,0:T(8,128)S(1)}, f32[16,8,4096]{2,1,0:T(8,128)}, u32[]{:S(2)}) copy-start(f32[16,8,4096]{2,1,0:T(8,128)} %param.10) | copy-start | bytes 6291460
  10.8 25.5 %copy-start.22 = (s32[8,4096]{1,0:T(8,128)S(1)}, s32[8,4096]{1,0:T(8,128)}, u32[]{:S(2)}) copy-start(s32[8,4096]{1,0:T(8,128)} %param.19) | copy-start | bytes 393220
  10.8 31.6 %copy-start.17 = (f32[8,4096]{1,0:T(8,128)S(1)}, f32[8,4096]{1,0:T(8,128)}, u32[]{:S(2)}) copy-start(f32[8,4096]{1,0:T(8,128)} %param.17) | copy-start | bytes 393220
  37.0 23.5 %collective-permute-start.12 = (f32[1,4096]{1,0:T(1,128)S(1)}, f32[1,4096]{1,0:T(1,128)S(1)}, u32[]{:S(2)}, u32[]{:S(2)}) collective-permute-start(f32[1,4096]{1,0:T(1,128)S(1)} %get-tuple-element.137), channel_id=1, source_target_pairs={{4,0},{8,4},{12,8},{16,12},{20,16},{24,20},{28,24},{5,1},{9,5},{13... | collective-permute-start | bytes 49160 | tf_op jit(solution)/shard_map/ppermute | solution.py:25
  40.1 24.0 %collective-permute-start.9 = (f32[1,4096]{1,0:T(1,128)}, f32[1,4096]{1,0:T(1,128)}, u32[]{:S(2)}, u32[]{:S(2)}) collective-permute-start(f32[1,4096]{1,0:T(1,128)} %get-tuple-element.138), channel_id=1, source_target_pairs={{0,4},{4,8},{8,12},{12,16},{16,20},{20,24},{24,28},{1,5},{5,9},{9,... | collective-permute-start | bytes 49160 | tf_op jit(solution)/shard_map/ppermute | solution.py:24
  43.0 25.1 %collective-permute-start.10 = (f32[1,4096]{1,0:T(1,128)}, f32[1,4096]{1,0:T(1,128)S(1)}, u32[]{:S(2)}, u32[]{:S(2)}) collective-permute-start(f32[1,4096]{1,0:T(1,128)} %get-tuple-element.140), channel_id=1, source_target_pairs={{0,4},{4,8},{8,12},{12,16},{16,20},{20,24},{24,28},{1,5},{5,9},{9,... | collective-permute-start | bytes 49160 | tf_op jit(solution)/shard_map/ppermute | solution.py:24
  47.7 22.6 %collective-permute-start.11 = (f32[1,4096]{1,0:T(1,128)}, f32[1,4096]{1,0:T(1,128)}, u32[]{:S(2)}, u32[]{:S(2)}) collective-permute-start(f32[1,4096]{1,0:T(1,128)} %get-tuple-element.135), channel_id=1, source_target_pairs={{4,0},{8,4},{12,8},{16,12},{20,16},{24,20},{28,24},{5,1},{9,5},{13... | collective-permute-start | bytes 49160 | tf_op jit(solution)/shard_map/ppermute | solution.py:25
  49.8 23.6 %collective-permute-start.13 = (f32[1,4096]{1,0:T(1,128)}, f32[1,4096]{1,0:T(1,128)}, u32[]{:S(2)}, u32[]{:S(2)}) collective-permute-start(f32[1,4096]{1,0:T(1,128)} %get-tuple-element.139), channel_id=1, source_target_pairs={{4,0},{8,4},{12,8},{16,12},{20,16},{24,20},{28,24},{5,1},{9,5},{13... | collective-permute-start | bytes 49160 | tf_op jit(solution)/shard_map/ppermute | solution.py:25
  61.1 12.3 %collective-permute-start.8 = (f32[1,4096]{1,0:T(1,128)}, f32[1,4096]{1,0:T(1,128)S(1)}, u32[]{:S(2)}, u32[]{:S(2)}) collective-permute-start(f32[1,4096]{1,0:T(1,128)} %get-tuple-element.136), channel_id=1, source_target_pairs={{0,4},{4,8},{8,12},{12,16},{16,20},{20,24},{24,28},{1,5},{5,9},{9,... | collective-permute-start | bytes 49160 | tf_op jit(solution)/shard_map/ppermute | solution.py:24
  64.1 41.4 %collective-permute-start = (f32[16,1,4096]{2,1,0:T(1,128)}, f32[16,1,4096]{2,1,0:T(1,128)}, u32[]{:S(2)}, u32[]{:S(2)}) collective-permute-start(f32[16,1,4096]{2,1,0:T(1,128)} %get-tuple-element.108), channel_id=1, source_target_pairs={{0,4},{4,8},{8,12},{12,16},{16,20},{20,24},{24,28},{1,5},{5,9},{9,... | collective-permute-start | bytes 786440 | tf_op jit(solution)/shard_map/ppermute | solution.py:24
  68.1 37.4 %collective-permute-start.1 = (f32[16,1,4096]{2,1,0:T(1,128)}, f32[16,1,4096]{2,1,0:T(1,128)}, u32[]{:S(2)}, u32[]{:S(2)}) collective-permute-start(f32[16,1,4096]{2,1,0:T(1,128)} %get-tuple-element.109), channel_id=1, source_target_pairs={{4,0},{8,4},{12,8},{16,12},{20,16},{24,20},{28,24},{5,1},{9,5},{13... | collective-permute-start | bytes 786440 | tf_op jit(solution)/shard_map/ppermute | solution.py:25
  70.3 46.6 %collective-permute-start.4 = (f32[16,1,4096]{2,1,0:T(1,128)}, f32[16,1,4096]{2,1,0:T(1,128)}, u32[]{:S(2)}, u32[]{:S(2)}) collective-permute-start(f32[16,1,4096]{2,1,0:T(1,128)} %get-tuple-element.110), channel_id=1, source_target_pairs={{0,4},{4,8},{8,12},{12,16},{16,20},{20,24},{24,28},{1,5},{5,9},{9,... | collective-permute-start | bytes 786440 | tf_op jit(solution)/shard_map/ppermute | solution.py:24
  78.1 6.4 %collective-permute-start.14 = (f32[1,4096]{1,0:T(1,128)S(1)}, f32[1,4096]{1,0:T(1,128)S(1)}, u32[]{:S(2)}, u32[]{:S(2)}) collective-permute-start(f32[1,4096]{1,0:T(1,128)S(1)} %get-tuple-element.128), channel_id=1, source_target_pairs={{0,4},{4,8},{8,12},{12,16},{16,20},{20,24},{24,28},{1,5},{5,9},{9,... | collective-permute-start | bytes 49160 | tf_op jit(solution)/shard_map/ppermute | solution.py:24
  81.4 5.2 %collective-permute-start.15 = (f32[1,4096]{1,0:T(1,128)S(1)}, f32[1,4096]{1,0:T(1,128)S(1)}, u32[]{:S(2)}, u32[]{:S(2)}) collective-permute-start(f32[1,4096]{1,0:T(1,128)S(1)} %get-tuple-element.129), channel_id=1, source_target_pairs={{4,0},{8,4},{12,8},{16,12},{20,16},{24,20},{28,24},{5,1},{9,5},{13... | collective-permute-start | bytes 49160 | tf_op jit(solution)/shard_map/ppermute | solution.py:25
  86.8 6.3 %collective-permute-start.16 = (f32[1,4096]{1,0:T(1,128)S(1)}, f32[1,4096]{1,0:T(1,128)S(1)}, u32[]{:S(2)}, u32[]{:S(2)}) collective-permute-start(f32[1,4096]{1,0:T(1,128)S(1)} %get-tuple-element.124), channel_id=1, source_target_pairs={{0,4},{4,8},{8,12},{12,16},{16,20},{20,24},{24,28},{1,5},{5,9},{9,... | collective-permute-start | bytes 49160 | tf_op jit(solution)/shard_map/ppermute | solution.py:24
  90.2 4.5 %collective-permute-start.17 = (f32[1,4096]{1,0:T(1,128)S(1)}, f32[1,4096]{1,0:T(1,128)S(1)}, u32[]{:S(2)}, u32[]{:S(2)}) collective-permute-start(f32[1,4096]{1,0:T(1,128)S(1)} %get-tuple-element.125), channel_id=1, source_target_pairs={{4,0},{8,4},{12,8},{16,12},{20,16},{24,20},{28,24},{5,1},{9,5},{13... | collective-permute-start | bytes 49160 | tf_op jit(solution)/shard_map/ppermute | solution.py:25
  94.9 6.3 %collective-permute-start.18 = (f32[1,4096]{1,0:T(1,128)S(1)}, f32[1,4096]{1,0:T(1,128)S(1)}, u32[]{:S(2)}, u32[]{:S(2)}) collective-permute-start(f32[1,4096]{1,0:T(1,128)S(1)} %get-tuple-element.119), channel_id=1, source_target_pairs={{0,4},{4,8},{8,12},{12,16},{16,20},{20,24},{24,28},{1,5},{5,9},{9,... | collective-permute-start | bytes 49160 | tf_op jit(solution)/shard_map/ppermute | solution.py:24
  99.2 4.8 %collective-permute-start.19 = (f32[1,4096]{1,0:T(1,128)S(1)}, f32[1,4096]{1,0:T(1,128)S(1)}, u32[]{:S(2)}, u32[]{:S(2)}) collective-permute-start(f32[1,4096]{1,0:T(1,128)S(1)} %get-tuple-element.118), channel_id=1, source_target_pairs={{4,0},{8,4},{12,8},{16,12},{20,16},{24,20},{28,24},{5,1},{9,5},{13... | collective-permute-start | bytes 49160 | tf_op jit(solution)/shard_map/ppermute | solution.py:25
  101.2 15.6 %collective-permute-start.5 = (f32[16,1,4096]{2,1,0:T(1,128)S(1)}, f32[16,1,4096]{2,1,0:T(1,128)S(1)}, u32[]{:S(2)}, u32[]{:S(2)}) collective-permute-start(f32[16,1,4096]{2,1,0:T(1,128)S(1)} %copy-done.21), channel_id=1, source_target_pairs={{4,0},{8,4},{12,8},{16,12},{20,16},{24,20},{28,24},{5,1},{9,5},{13... | collective-permute-start | bytes 786440 | tf_op jit(solution)/shard_map/ppermute | solution.py:25
  106.4 19.6 %collective-permute-start.2 = (f32[1,10,4096]{2,1,0:T(8,128)S(1)}, f32[1,10,4096]{2,1,0:T(8,128)S(1)}, u32[]{:S(2)}, u32[]{:S(2)}) collective-permute-start(f32[1,10,4096]{2,1,0:T(8,128)S(1)} %get-tuple-element.77), channel_id=1, source_target_pairs={{0,1},{1,2},{2,3},{4,5},{5,6},{6,7},{8,9},{9,10},{10,11},{12,13},{... | collective-permute-start | bytes 491528 | tf_op jit(solution)/shard_map/ppermute | solution.py:24
  107.7 18.3 %collective-permute-start.3 = (f32[1,10,4096]{2,1,0:T(8,128)S(1)}, f32[1,10,4096]{2,1,0:T(8,128)S(1)}, u32[]{:S(2)}, u32[]{:S(2)}) collective-permute-start(f32[1,10,4096]{2,1,0:T(8,128)S(1)} %get-tuple-element.78), channel_id=1, source_target_pairs={{1,0},{2,1},{3,2},{5,4},{6,5},{7,6},{9,8},{10,9},{11,10},{13,12},{... | collective-permute-start | bytes 491528 | tf_op jit(solution)/shard_map/ppermute | solution.py:25
  117.7 8.3 %collective-permute-start.6 = (f32[1,10,4096]{2,1,0:T(8,128)S(1)}, f32[1,10,4096]{2,1,0:T(8,128)S(1)}, u32[]{:S(2)}, u32[]{:S(2)}) collective-permute-start(f32[1,10,4096]{2,1,0:T(8,128)S(1)} %get-tuple-element.79), channel_id=1, source_target_pairs={{0,1},{1,2},{2,3},{4,5},{5,6},{6,7},{8,9},{9,10},{10,11},{12,13},{... | collective-permute-start | bytes 491528 | tf_op jit(solution)/shard_map/ppermute | solution.py:24
  119.0 7.0 %collective-permute-start.7 = (f32[1,10,4096]{2,1,0:T(8,128)S(1)}, f32[1,10,4096]{2,1,0:T(8,128)S(1)}, u32[]{:S(2)}, u32[]{:S(2)}) collective-permute-start(f32[1,10,4096]{2,1,0:T(8,128)S(1)} %get-tuple-element.80), channel_id=1, source_target_pairs={{1,0},{2,1},{3,2},{5,4},{6,5},{7,6},{9,8},{10,9},{11,10},{13,12},{... | collective-permute-start | bytes 491528 | tf_op jit(solution)/shard_map/ppermute | solution.py:25
  (25 other events, 200.9 us)
Sparse Core Ops, SparseCore 0:
  36.4 30.8 all-reduce.16
where the time goes:
time: 229 us; the launch traced here: 227 us
  other arithmetic  81.6 us (36%)
  starting transfers between devices  63.8 us (28%)
  blocking collectives  46.6 us (20%)
  local copies, waits for them, and re-layouts  16.5 us (7%)
  between operations  15 us (7%)
  waiting for transfers between devices  3.75 us (2%)
    ppermute x10, starting transfers between devices, with_halo(): after = lax.ppermute(initial, axis, down)  34.5 us
    ppermute x10, starting transfers between devices, with_halo(): before = lax.ppermute(last, axis, up)  29.2 us
    another operation x3, other arithmetic, per_device(): stacked_rhs = jnp.stack([-residual, coupling_up, coupling_down], axis=1)  24.6 us
    mul x1, other arithmetic, soil_state(): conductivity = saturated * wetness  23.3 us
    add x1, other arithmetic, newton_system(): diagonal = capacity / TIME_STEP + vface[:-1] + vface[1:]  10.9 us
    all_gather x1, blocking collectives, per_device(): lax.all_gather(pieces[0][None], 'depth', axis=0, tiled=True)  10.2 us
    all_gather x1, blocking collectives, per_device(): lax.all_gather(pieces[1][None], 'depth', axis=0, tiled=True)  7.29 us
    all_gather x1, blocking collectives, per_device(): lax.all_gather(pieces[4][None], 'depth', axis=0, tiled=True)  7.28 us
  transfers between devices with their start and end apart: 21, of which 2 were waited for; matrix products, arithmetic and copies ran while one was open for 9% of the time, Pallas kernels for 0%

commit v1 on v0

v1 whole, which is shorter than its diff:
```python
import functools

import jax
import jax.numpy as jnp
from jax import lax
from jax.experimental import pallas as pl
from jax.experimental.pallas import tpu as pltpu
from jax.sharding import PartitionSpec as P

SWEEPS = 4
TIME_STEP = 20.0
SURFACE_STEP = 2.0
SPECIFIC_STORAGE = 0.01
LAND_CONVEYANCE = 3.0
RIVER_CONVEYANCE = 10.0
SLOPE_FLOOR = 0.01
PAD = 128
TINY = 1e-30
MESH = pl.DeviceIdType.MESH


def recip(value):
    guess = pl.reciprocal(value, approx=True)
    return guess * (2.0 - value * guess)


def harmonic(first, second):
    return 2.0 * first * second * recip(jnp.maximum(first + second, TINY))


def lookup(soil, tables):
    masks = [soil == kind for kind in range(1, tables[0].shape[0])]
    found = []
    for table in tables:
        value = jnp.full(soil.shape, table[0], jnp.float32)
        for kind, mask in enumerate(masks):
            value = jnp.where(mask, table[kind + 1], value)
        found.append(value)
    return found


def face_k(depth_face, slope, conveyance):
    power = jnp.exp((5.0 / 3.0) * jnp.log(jnp.maximum(depth_face, TINY)))
    return power * conveyance * lax.rsqrt(jnp.abs(slope) + SLOPE_FLOOR)


def kernel(
    sizes, head, head_old, soil, cond_t, shape_t, pore_t, pond, ground, ponded, river,
    out, surf,
    head_x, cond_x, old_v, soil_v, base_v, capd_v, y_v, r_v, out_v,
    bsend, bsoil, lrecv, flux_v, nsend, m2recv, m3recv, m4send, m4recv,
    top_v, xrecv, pack, srecv, sext, lev_v,
    in_sem, row_sem, out_sem, lat_s, lat_r, m1_s, m1_r, n_s, m2_r, m3_r, m4_s, m4_r,
    x_s, x_r, surf_s, surf_r,
):
    layers, rows, width, lat_count, chunk = sizes
    count = width // chunk
    strip = width // 4
    window = min(strip + 2 * PAD, width)
    lat = lax.axis_index("lat")
    depth = lax.axis_index("depth")
    has_up = lat > 0
    has_down = lat < lat_count - 1
    top_half = depth < 2
    is_top = depth == 0
    outer = (depth == 0) | (depth == 3)
    inner = (depth == 1) | (depth == 2)
    partner = jnp.where(top_half, 1 - depth, 5 - depth)
    middle = 3 - depth
    sign = jnp.where(top_half, 1.0, -1.0).astype(jnp.float32)
    stride = jnp.where(top_half, 1, -1)

    def layer_at(place):
        return jnp.where(top_half, place, layers - 1 - place)

    def start_of(index):
        return jnp.clip(index * strip - PAD, 0, width - window)

    body = pl.ds(PAD, width)
    loads = (
        pltpu.make_async_copy(head, head_x.at[pl.ds(1, layers), :, body], in_sem.at[0]),
        pltpu.make_async_copy(soil, soil_v, in_sem.at[1]),
        pltpu.make_async_copy(head_old, old_v, in_sem.at[2]),
    )
    row_loads = []
    for side, row in ((0, 0), (1, rows - 1)):
        row_loads.append(pltpu.make_async_copy(head.at[:, row, :], bsend.at[side, 0], row_sem.at[side, 0]))
        row_loads.append(pltpu.make_async_copy(soil.at[:, row, :], bsoil.at[side], row_sem.at[side, 1]))
    for copy in row_loads:
        copy.start()
    for copy in loads:
        copy.start()

    barrier = pltpu.get_barrier_semaphore()
    for shift in range(1, 4):
        pl.semaphore_signal(barrier, inc=1, device_id={"depth": lax.rem(depth + shift, 4)}, device_id_type=MESH)

    @pl.when(has_up)
    def _():
        pl.semaphore_signal(barrier, inc=1, device_id={"lat": lat - 1}, device_id_type=MESH)

    @pl.when(has_down)
    def _():
        pl.semaphore_signal(barrier, inc=1, device_id={"lat": lat + 1}, device_id_type=MESH)

    zero_pad = jnp.zeros((layers + 2, rows, PAD), jnp.float32)
    for field in (head_x, cond_x):
        field[:, :, pl.ds(0, PAD)] = zero_pad
        field[:, :, pl.ds(PAD + width, PAD)] = zero_pad

    for side, present in ((0, has_up), (1, has_down)):
        @pl.when(jnp.logical_not(present))
        def _():
            lrecv[side] = jnp.zeros(lrecv.shape[1:], jnp.float32)
            srecv[side] = jnp.zeros(srecv.shape[1:], jnp.float32)

    pl.semaphore_wait(barrier, 3 + jnp.where(has_up, 1, 0) + jnp.where(has_down, 1, 0))

    def lat_copy(side, index):
        cols = pl.ds(pl.multiple_of(index * chunk, 128), chunk)
        return pltpu.make_async_remote_copy(
            src_ref=bsend.at[side, :, :, cols],
            dst_ref=lrecv.at[1 - side, :, :, cols],
            send_sem=lat_s.at[side, index],
            recv_sem=lat_r.at[1 - side, index],
            device_id={"lat": lat - 1 if side == 0 else lat + 1},
            device_id_type=MESH,
        )

    def lat_arrival(side, index):
        cols = pl.ds(pl.multiple_of(index * chunk, 128), chunk)
        return pltpu.make_async_remote_copy(
            src_ref=bsend.at[1 - side, :, :, cols],
            dst_ref=lrecv.at[side, :, :, cols],
            send_sem=lat_s.at[1 - side, index],
            recv_sem=lat_r.at[side, index],
            device_id={"lat": lat - 1 if side == 0 else lat + 1},
            device_id_type=MESH,
        )

    for copy in row_loads:
        copy.wait()

    def boundary(index, carry):
        cols = pl.ds(pl.multiple_of(index * chunk, 128), chunk)
        for side, present in ((0, has_up), (1, has_down)):
            saturated, steep = lookup(bsoil[side, :, cols], (cond_t, shape_t))
            bsend[side, 1, :, cols] = saturated * jnp.exp(steep * jnp.minimum(bsend[side, 0, :, cols], 0.0))

            @pl.when(present)
            def _():
                lat_copy(side, index).start()
        return carry

    lax.fori_loop(0, count, boundary, 0)

    for copy in loads:
        copy.wait()

    def end_layer(layer):
        def step(index, carry):
            cols = pl.ds(pl.multiple_of(index * chunk, 128), chunk)
            wide = pl.ds(pl.multiple_of(index * chunk + PAD, 128), chunk)
            saturated, steep = lookup(soil_v[layer, :, cols], (cond_t, shape_t))
            cond_x[layer + 1, :, wide] = saturated * jnp.exp(steep * jnp.minimum(head_x[layer + 1, :, wide], 0.0))
            return carry
        lax.fori_loop(0, count, step, 0)

    def m1_copy(place, target):
        slot = jnp.where(top_half, layers + 1, 0) if place == 0 else jnp.where(top_half, 0, layers + 1)
        layer = layer_at(0 if place == 0 else layers - 1) + 1
        return [
            pltpu.make_async_remote_copy(
                src_ref=field.at[layer, :, body],
                dst_ref=field.at[slot, :, body],
                send_sem=m1_s.at[place, which],
                recv_sem=m1_r.at[which],
                device_id={"depth": target},
                device_id_type=MESH,
            )
            for which, field in enumerate((head_x, cond_x))
        ]

    def m1_arrival():
        slot = jnp.where(top_half, layers + 1, 0)
        layer = layer_at(layers - 1) + 1
        return [
            pltpu.make_async_remote_copy(
                src_ref=field.at[layer, :, body],
                dst_ref=field.at[slot, :, body],
                send_sem=m1_s.at[1, which],
                recv_sem=m1_r.at[which],
                device_id={"depth": partner},
                device_id_type=MESH,
            )
            for which, field in enumerate((head_x, cond_x))
        ]

    @pl.when(inner)
    def _():
        end_layer(layer_at(layers - 1))
        for copy in m1_copy(1, middle):
            copy.start()
        end_layer(layer_at(0))
        for copy in m1_copy(0, partner):
            copy.start()

    def x_copy(target):
        return pltpu.make_async_remote_copy(
            src_ref=top_v.at[:, pl.ds(min(max(target * strip - PAD, 0), width - window), window)],
            dst_ref=xrecv,
            send_sem=x_s.at[target],
            recv_sem=x_r,
            device_id={"depth": target},
            device_id_type=MESH,
        )

    @pl.when(is_top)
    def _():
        end_layer(0)
        wet = ponded[...].astype(jnp.float32) * pond[...]
        top_v[...] = cond_x[1, :, body] * (2.0 * (wet - head_x[1, :, body]) + 1.0)
        for target in range(1, 4):
            x_copy(target).start()
        xrecv[...] = top_v[:, pl.ds(0, window)]

    def state(index, carry):
        layer = index // count
        begin = lax.rem(index, count) * chunk
        cols = pl.ds(pl.multiple_of(begin, 128), chunk)
        wide = pl.ds(pl.multiple_of(begin + PAD, 128), chunk)
        saturated, steep, pore = lookup(soil_v[layer, :, cols], (cond_t, shape_t, pore_t))
        now = head_x[layer + 1, :, wide]
        old = old_v[layer, :, cols]
        wet = jnp.exp(steep * jnp.minimum(now, 0.0))
        wet_old = jnp.exp(steep * jnp.minimum(old, 0.0))
        value = saturated * wet

        already = (inner & ((layer == 0) | (layer == layers - 1))) | (is_top & (layer == 0))

        @pl.when(jnp.logical_not(already))
        def _():
            cond_x[layer + 1, :, wide] = value

        base_v[layer, :, cols] = (pore * (wet - wet_old) + SPECIFIC_STORAGE * (now - old)) * (1.0 / TIME_STEP)
        capd_v[layer, :, cols] = (SPECIFIC_STORAGE + pore * steep * wet) * (1.0 / TIME_STEP)
        return carry

    lax.fori_loop(0, layers * count, state, 0)

    @pl.when(jnp.logical_not(is_top))
    def _():
        x_copy(1).wait_recv()

    begin = pl.multiple_of(start_of(depth), 128)
    view = pl.ds(begin, window)
    conveyance = LAND_CONVEYANCE + (RIVER_CONVEYANCE - LAND_CONVEYANCE) * river[:, view].astype(jnp.float32)
    own = (pond[:, view], ground[:, view], conveyance, -xrecv[...])
    for place, value in enumerate(own):
        for side, first in ((0, 0), (1, rows - 4)):
            pack[side, pl.ds(4 * place, 4), :] = value[first:first + 4]
        sext[place, pl.ds(4, rows), :] = value

    def surf_copy(side):
        return pltpu.make_async_remote_copy(
            src_ref=pack.at[side],
            dst_ref=srecv.at[1 - side],
            send_sem=surf_s.at[side],
            recv_sem=surf_r.at[1 - side],
            device_id={"lat": lat - 1 if side == 0 else lat + 1},
            device_id_type=MESH,
        )

    def surf_arrival(side):
        return pltpu.make_async_remote_copy(
            src_ref=pack.at[1 - side],
            dst_ref=srecv.at[side],
            send_sem=surf_s.at[1 - side],
            recv_sem=surf_r.at[side],
            device_id={"lat": lat - 1 if side == 0 else lat + 1},
            device_id_type=MESH,
        )

    for side, present in ((0, has_up), (1, has_down)):
        @pl.when(present)
        def _():
            surf_copy(side).start()

    def surface():
        for side, present in ((0, has_up), (1, has_down)):
            @pl.when(present)
            def _():
                surf_arrival(side).wait_recv()
        for place in range(4):
            sext[place, pl.ds(0, 4), :] = srecv[0, pl.ds(4 * place, 4), :]
            sext[place, pl.ds(4 + rows, 4), :] = srecv[1, pl.ds(4 * place, 4), :]
        tall = rows + 8
        depth_w, ground_w, conv_w, exfil = (sext[place] for place in range(4))
        row = lax.broadcasted_iota(jnp.int32, (tall, window), 0)
        col = lax.broadcasted_iota(jnp.int32, (tall, window), 1)

        def after(value, axis):
            return pltpu.roll(value, value.shape[axis] - 1, axis)

        def before(value, axis):
            return pltpu.roll(value, 1, axis)

        total = jnp.full((tall, window), 1.0 / SURFACE_STEP, jnp.float32)
        rhs = depth_w * (1.0 / SURFACE_STEP) + exfil
        faces = []
        for axis, last in ((0, row == tall - 1), (1, col == window - 1)):
            depth_n, ground_n, conv_n = (after(value, axis) for value in (depth_w, ground_w, conv_w))
            k = face_k(
                0.5 * (depth_w + depth_n),
                depth_n + ground_n - (depth_w + ground_w),
                harmonic(conv_w, conv_n),
            )
            k = jnp.where(last, 0.0, k)
            k_before = before(k, axis)
            flow = k * (ground_n - ground_w)
            total = total + k + k_before
            rhs = rhs + flow - before(flow, axis)
            faces.append((axis, k, k_before))
        scale = recip(total)
        level = depth_w
        for _ in range(SWEEPS):
            fed = rhs
            for axis, k, k_before in faces:
                fed = fed + k * after(level, axis) + k_before * before(level, axis)
            level = fed * scale
        lev_v[...] = level[4:4 + rows]
        offset = pl.multiple_of(depth * strip - begin, 128)
        surf[...] = lev_v[:, pl.ds(offset, strip)]

    def m2_copy(index):
        cols = pl.ds(pl.multiple_of(index * chunk, 128), chunk)
        return pltpu.make_async_remote_copy(
            src_ref=nsend.at[:, :, cols], dst_ref=m2recv.at[:, :, cols],
            send_sem=n_s.at[index], recv_sem=m2_r.at[index],
            device_id={"depth": partner}, device_id_type=MESH,
        )

    def m3_copy(index):
        cols = pl.ds(pl.multiple_of(index * chunk, 128), chunk)
        return pltpu.make_async_remote_copy(
            src_ref=nsend.at[:, :, cols], dst_ref=m3recv.at[:, :, cols],
            send_sem=n_s.at[index], recv_sem=m3_r.at[index],
            device_id={"depth": middle}, device_id_type=MESH,
        )

    def m4_copy(index):
        cols = pl.ds(pl.multiple_of(index * chunk, 128), chunk)
        return pltpu.make_async_remote_copy(
            src_ref=m4send.at[:, cols], dst_ref=m4recv.at[:, cols],
            send_sem=m4_s.at[index], recv_sem=m4_r.at[index],
            device_id={"depth": partner}, device_id_type=MESH,
        )

    def out_copy(index):
        cols = pl.ds(pl.multiple_of(index * chunk, 128), chunk)
        return pltpu.make_async_copy(out_v.at[:, :, cols], out.at[:, :, cols], out_sem.at[index])

    for copy in m1_arrival():
        copy.wait_recv()

    row8 = lax.broadcasted_iota(jnp.int32, (rows, chunk), 0)

    def eliminate(index):
        cols = pl.ds(pl.multiple_of(index * chunk, 128), chunk)
        mid = pl.ds(pl.multiple_of(index * chunk + PAD, 128), chunk)
        wide = pl.ds(pl.multiple_of(index * chunk, 128), chunk + 2 * PAD)
        for side, present in ((0, has_up), (1, has_down)):
            @pl.when(present)
            def _():
                lat_arrival(side, index).wait_recv()
            mine_h, mine_c = bsend[side, 0, :, cols], bsend[side, 1, :, cols]
            theirs_h, theirs_c = lrecv[side, 0, :, cols], lrecv[side, 1, :, cols]
            flux_v[side] = harmonic(mine_c, theirs_c) * (theirs_h - mine_h)

        @pl.when(outer)
        def _():
            layer = layer_at(0) + 1
            first = cond_x[layer, :, mid]
            wet = ponded[:, cols].astype(jnp.float32) * pond[:, cols]
            inflow = first * (2.0 * (wet - head_x[layer, :, mid]) + 1.0)
            m2recv[0, :, cols] = jnp.where(is_top, 2.0 * first, 0.0)
            m2recv[1, :, cols] = jnp.where(is_top, inflow, -first)

        @pl.when(inner)
        def _():
            m2_copy(index).wait_recv()

        def step(place, carry):
            extra, inflow = carry
            layer = layer_at(place)
            slot = layer + 1
            cond_w = cond_x[slot, :, wide]
            head_w = head_x[slot, :, wide]
            cond = cond_w[:, PAD:PAD + chunk]
            here = head_w[:, PAD:PAD + chunk]
            face = harmonic(cond, cond_x[slot + stride, :, mid])
            flux = face * (here - head_x[slot + stride, :, mid] + sign)
            size = chunk + 2 * PAD
            cond_a = pltpu.roll(cond_w, size - 1, 1)[:, :chunk + PAD]
            head_a = pltpu.roll(head_w, size - 1, 1)[:, :chunk + PAD]
            along = harmonic(cond_w[:, :chunk + PAD], cond_a) * (head_a - head_w[:, :chunk + PAD])
            lateral = along[:, PAD:] - pltpu.roll(along, 1, 1)[:, PAD:]
            across = harmonic(cond, pltpu.roll(cond, rows - 1, 0)) * (pltpu.roll(here, rows - 1, 0) - here)
            across = jnp.where(row8 == rows - 1, 0.0, across)
            lateral = lateral + across - pltpu.roll(across, 1, 0)
            above = flux_v[0, pl.ds(layer, 1), :]
            below = flux_v[1, pl.ds(layer, 1), :]
            lateral = lateral + jnp.where(row8 == 0, above, jnp.where(row8 == rows - 1, below, 0.0))
            scale = recip(capd_v[layer, :, cols] + face + extra)
            ratio = face * scale
            value = (inflow - flux - base_v[layer, :, cols] + lateral) * scale
            y_v[place, :, cols] = value
            r_v[place, :, cols] = ratio
            return (face - face * ratio, flux + face * value)

        extra, inflow = lax.fori_loop(0, layers, step, (m2recv[0, :, cols], m2recv[1, :, cols]))
        nsend[0, :, cols] = jnp.where(outer, extra, y_v[layers - 1, :, cols])
        nsend[1, :, cols] = jnp.where(outer, inflow, r_v[layers - 1, :, cols])

        @pl.when(outer)
        def _():
            m2_copy(index).start()

        @pl.when(inner)
        def _():
            m3_copy(index).start()

    def substitute(index, beyond):
        cols = pl.ds(pl.multiple_of(index * chunk, 128), chunk)
        mid = pl.ds(pl.multiple_of(index * chunk + PAD, 128), chunk)

        def step(place, found):
            place = layers - 1 - place
            layer = layer_at(place)
            found = y_v[place, :, cols] + r_v[place, :, cols] * found
            out_v[layer, :, cols] = head_x[layer + 1, :, mid] + found
            return found

        found = lax.fori_loop(0, layers, step, beyond)
        out_copy(index).start()
        return found

    def finish_inner(index):
        cols = pl.ds(pl.multiple_of(index * chunk, 128), chunk)
        m3_copy(index).wait_recv()
        y_own, r_own = nsend[0, :, cols], nsend[1, :, cols]
        y_far, r_far = m3recv[0, :, cols], m3recv[1, :, cols]
        m4send[:, cols] = substitute(index, (y_far + r_far * y_own) * recip(1.0 - r_own * r_far))
        m4_copy(index).start()

    def finish_outer(index):
        cols = pl.ds(pl.multiple_of(index * chunk, 128), chunk)
        m4_copy(index).wait_recv()
        substitute(index, m4recv[:, cols])

    def turn(index, carry):
        @pl.when(index < count)
        def _():
            eliminate(index)

        @pl.when(index == count)
        def _():
            surface()

        @pl.when(inner & (index >= 1) & (index <= count))
        def _():
            finish_inner(index - 1)

        @pl.when(outer & (index >= 2))
        def _():
            finish_outer(index - 2)

        return carry

    lax.fori_loop(0, count + 2, turn, 0)

    def drain(index, carry):
        for side, present in ((0, has_up), (1, has_down)):
            @pl.when(present)
            def _():
                lat_copy(side, index).wait_send()

        @pl.when(outer)
        def _():
            m2_copy(index).wait_send()

        @pl.when(inner)
        def _():
            m3_copy(index).wait_send()
            m4_copy(index).wait_send()

        out_copy(index).wait()
        return carry

    lax.fori_loop(0, count, drain, 0)
    for side, present in ((0, has_up), (1, has_down)):
        @pl.when(present)
        def _():
            surf_copy(side).wait_send()

    @pl.when(inner)
    def _():
        for copy in m1_copy(1, middle) + m1_copy(0, partner):
            copy.wait_send()

    @pl.when(is_top)
    def _():
        for target in range(1, 4):
            x_copy(target).wait_send()


def per_device(lat_count, chunk, head, head_old, soil, cond_t, shape_t, pore_t, pond, ground, ponded, river):
    layers, rows, width = head.shape
    chunk = min(chunk, width)
    count = width // chunk
    strip = width // 4
    window = min(strip + 2 * PAD, width)
    f32 = jnp.float32
    padded = (layers + 2, rows, width + 2 * PAD)
    full = (layers, rows, width)
    plane = (rows, width)
    pair = (2, rows, width)
    any_spec = pl.BlockSpec(memory_space=pl.ANY)
    smem = pl.BlockSpec(memory_space=pltpu.SMEM)
    vmem = pl.BlockSpec(memory_space=pltpu.VMEM)
    dma = pltpu.SemaphoreType.DMA
    return pl.pallas_call(
        functools.partial(kernel, (layers, rows, width, lat_count, chunk)),
        out_shape=(jax.ShapeDtypeStruct(full, f32), jax.ShapeDtypeStruct((rows, strip), f32)),
        in_specs=[any_spec] * 3 + [smem] * 3 + [vmem] * 4,
        out_specs=(any_spec, vmem),
        scratch_shapes=[
            pltpu.VMEM(padded, f32),
            pltpu.VMEM(padded, f32),
            pltpu.VMEM(full, f32),
            pltpu.VMEM(full, jnp.int32),
            pltpu.VMEM(full, f32),
            pltpu.VMEM(full, f32),
            pltpu.VMEM(full, f32),
            pltpu.VMEM(full, f32),
            pltpu.VMEM(full, f32),
            pltpu.VMEM((2, 2, layers, width), f32),
            pltpu.VMEM((2, layers, width), jnp.int32),
            pltpu.VMEM((2, 2, layers, width), f32),
            pltpu.VMEM((2, layers, chunk), f32),
            pltpu.VMEM(pair, f32),
            pltpu.VMEM(pair, f32),
            pltpu.VMEM(pair, f32),
            pltpu.VMEM(plane, f32),
            pltpu.VMEM(plane, f32),
            pltpu.VMEM(plane, f32),
            pltpu.VMEM((rows, window), f32),
            pltpu.VMEM((2, 16, window), f32),
            pltpu.VMEM((2, 16, window), f32),
            pltpu.VMEM((4, rows + 8, window), f32),
            pltpu.VMEM((rows, window), f32),
            dma((3,)),
            dma((2, 2)),
            dma((count,)),
            dma((2, count)),
            dma((2, count)),
            dma((2, 2)),
            dma((2,)),
            dma((count,)),
            dma((count,)),
            dma((count,)),
            dma((count,)),
            dma((count,)),
            dma((4,)),
            dma(()),
            dma((2,)),
            dma((2,)),
        ],
        compiler_params=pltpu.CompilerParams(
            collective_id=0, has_side_effects=True, vmem_limit_bytes=56 * 1024 * 1024
        ),
    )(head, head_old, soil, cond_t, shape_t, pore_t, pond, ground, ponded, river)


def solution(mesh):
    deep = P("depth", "lat", None)
    flat = P("lat", None)
    return jax.shard_map(
        functools.partial(per_device, mesh.shape["lat"], 512),
        mesh=mesh,
        in_specs=(deep, deep, deep, P(), P(), P(), flat, flat, flat, flat),
        out_specs=(deep, P("lat", "depth")),
        check_vma=False,
    )
```

time: 229 us -> 62 us (0.27)
  other arithmetic: 81.6 us -> 0 us
  starting transfers between devices: 63.8 us -> 0 us
  Pallas kernels: 0 us -> 57.5 us
  blocking collectives: 46.6 us -> 0 us
  between operations: 15 us -> 0.65 us
  local copies, waits for them, and re-layouts: 16.5 us -> 3.74 us
  waiting for transfers between devices: 3.75 us -> 0 us
    ppermute x20 -> x0, starting transfers between devices: 63.8 us -> none  [the longest x10 34.5 us: with_halo(): after = lax.ppermute(initial, axis, down)]
    pallas_call x0 -> x1, Pallas kernels: none -> 57.5 us  [per_device(): pl.pallas_call(functools.partial(kernel, (layers, rows, width, lat_count,...]
    all_gather x6 -> x0, blocking collectives: 46.6 us -> none  [the longest x1 10.2 us: per_device(): lax.all_gather(pieces[0][None], 'depth', axis=0, tiled=True)]
    mul x10 -> x0, other arithmetic: 27.9 us -> none  [the longest x1 23.3 us: soil_state(): conductivity = saturated * wetness]
    another operation x3 -> x0, other arithmetic: 24.6 us -> none  [per_device(): stacked_rhs = jnp.stack([-residual, coupling_up, coupling_down], axis=1)]
    add x6 -> x0, other arithmetic: 15.5 us -> none  [the longest x1 10.9 us: newton_system(): diagonal = capacity / TIME_STEP + vface[:-1] + vface[1:]]
    slice x17 -> x0, local copies, waits for them, and re-layouts: 11.4 us -> none  [the longest x4 4.82 us: with_halo(): last = lax.slice_in_dim(x, length - width, length, axis=dim)]
    div x7 -> x0, other arithmetic: 8.02 us -> none  [the longest x2 4.42 us: harmonic(): return 2.0 * first * second / jnp.where(total > 0.0, total, 1.0)]
  transfers between devices with their start and end apart: 21 -> 0, of which waited for: 2 -> 0; matrix products, arithmetic and copies ran while one was open for 9% -> 0% of each run, Pallas kernels for 0% -> 0%
where the time goes in v1:
time: 62 us; the launch traced here: 61.9 us
  Pallas kernels  57.5 us (93%)
  local copies, waits for them, and re-layouts  3.74 us (6%)
  between operations  0.65 us (1%)
    pallas_call x1, Pallas kernels, per_device(): pl.pallas_call(functools.partial(kernel, (layers, rows, width, lat_count,...  57.5 us
    unnamed x4, local copies, waits for them, and re-layouts  3.74 us

profile of v1, /device:TPU:13, one launch (start us, length us, event | category | flops | bytes accessed | tf_op | source)
XLA Modules:
  0.0 61.9 jit_solution(4459244627949857602)
XLA Ops:
  0.6 57.5 %shard_map.113 = (f32[16,8,4096]{2,1,0:T(8,128)}, f32[8,1024]{1,0:T(8,128)}) custom-call(f32[16,8,4096]{2,1,0:T(8,128)} %head.1, f32[16,8,4096]{2,1,0:T(8,128)} %head_old.1, s32[16,8,4096]{2,1,0:T(8,128)} %soil.1, f32[12]{0:T(128)} %cond_t.1, f32[12]{0:T(128)} %shape_t.1, f32[12]{0:T(128)} %pore_t.1, f32[8,4096]{1,0:T(8,128)} %pond.1, f32[8,4096]{1,0:T(8,128)} %ground.1, ...), custom_call_target="tpu_custom_call" | custom-call | tf_op jit(solution)/shard_map/pallas_call | solution.py:532
  58.1 0.0 copy-start
  58.1 3.1 %copy.14 = f32[16,8,4096]{2,1,0:T(8,128)} copy(f32[16,8,4096]{2,1,0:T(8,128)} %get-tuple-element.4) | data formatting | bytes 4194304
  61.2 0.0 copy-done
  61.2 0.6 copy.15
Async XLA Ops:
  58.1 3.1 %copy-start = (f32[8,1024]{1,0:T(8,128)S(1)}, f32[8,1024]{1,0:T(8,128)}, u32[]{:S(2)}) copy-start(f32[8,1024]{1,0:T(8,128)} %get-tuple-element.5) | copy-start | bytes 98308

commit v2 on v1

--- a/solution.py
+++ b/solution.py
@@ -16,6 +16,7 @@
 SLOPE_FLOOR = 0.01
 PAD = 128
 TINY = 1e-30
+CLOSED = 3e38
 MESH = pl.DeviceIdType.MESH
 
 
@@ -28,15 +29,29 @@
     return 2.0 * first * second * recip(jnp.maximum(first + second, TINY))
 
 
-def lookup(soil, tables):
-    masks = [soil == kind for kind in range(1, tables[0].shape[0])]
-    found = []
-    for table in tables:
-        value = jnp.full(soil.shape, table[0], jnp.float32)
-        for kind, mask in enumerate(masks):
-            value = jnp.where(mask, table[kind + 1], value)
-        found.append(value)
-    return found
+def lane_table(table, scale):
+    lane = lax.broadcasted_iota(jnp.int32, (8, 128), 1)
+    value = jnp.zeros((8, 128), jnp.float32)
+    for kind in range(table.shape[0]):
+        value = jnp.where(lane == kind, scale * table[kind], value)
+    return value
+
+
+def lookup(soil, table):
+    lines = []
+    for top in range(0, soil.shape[0], 8):
+        tiles = [
+            jnp.take_along_axis(
+                table, soil[top:top + 8, left:left + 128], axis=1, mode="promise_in_bounds"
+            )
+            for left in range(0, soil.shape[1], 128)
+        ]
+        lines.append(jnp.concatenate(tiles, axis=1))
+    return lines[0] if len(lines) == 1 else jnp.concatenate(lines, axis=0)
+
+
+def series(first, second):
+    return recip(first + second)
 
 
 def face_k(depth_face, slope, conveyance):
@@ -46,11 +61,11 @@
 
 def kernel(
     sizes, head, head_old, soil, cond_t, shape_t, pore_t, pond, ground, ponded, river,
-    out, surf,
-    head_x, cond_x, old_v, soil_v, base_v, capd_v, y_v, r_v, out_v,
-    bsend, bsoil, lrecv, flux_v, nsend, m2recv, m3recv, m4send, m4recv,
+    out_v, surf,
+    head_x, cond_x, old_v, soil_v, base_v, capd_v, face_v, rhs_v, sum_v, last_v, y_v, r_v,
+    bsend, lrecv, flux_v, nsend, m2recv, m3recv, m4send, m4recv,
     top_v, xrecv, pack, srecv, sext, lev_v,
-    in_sem, row_sem, out_sem, lat_s, lat_r, m1_s, m1_r, n_s, m2_r, m3_r, m4_s, m4_r,
+    in_sem, lat_s, lat_r, m1_s, m1_r, n_s, m2_r, m3_r, m4_s, m4_r,
     x_s, x_r, surf_s, surf_r,
 ):
     layers, rows, width, lat_count, chunk = sizes
@@ -77,19 +92,21 @@
         return jnp.clip(index * strip - PAD, 0, width - window)
 
     body = pl.ds(PAD, width)
-    loads = (
-        pltpu.make_async_copy(head, head_x.at[pl.ds(1, layers), :, body], in_sem.at[0]),
-        pltpu.make_async_copy(soil, soil_v, in_sem.at[1]),
-        pltpu.make_async_copy(head_old, old_v, in_sem.at[2]),
-    )
-    row_loads = []
-    for side, row in ((0, 0), (1, rows - 1)):
-        row_loads.append(pltpu.make_async_copy(head.at[:, row, :], bsend.at[side, 0], row_sem.at[side, 0]))
-        row_loads.append(pltpu.make_async_copy(soil.at[:, row, :], bsoil.at[side], row_sem.at[side, 1]))
-    for copy in row_loads:
-        copy.start()
-    for copy in loads:
-        copy.start()
+    def loads(part):
+        cols = pl.ds(pl.multiple_of(part * chunk, 128), chunk)
+        wide = pl.ds(pl.multiple_of(part * chunk + PAD, 128), chunk)
+        return (
+            pltpu.make_async_copy(head.at[:, :, cols], head_x.at[pl.ds(1, layers), :, wide], in_sem.at[0, part]),
+            pltpu.make_async_copy(soil.at[:, :, cols], soil_v.at[:, :, cols], in_sem.at[1, part]),
+            pltpu.make_async_copy(head_old.at[:, :, cols], old_v.at[:, :, cols], in_sem.at[2, part]),
+        )
+
+    def begin_loads(part, carry):
+        for copy in loads(part):
+            copy.start()
+        return carry
+
+    lax.fori_loop(0, count, begin_loads, 0)
 
     barrier = pltpu.get_barrier_semaphore()
     for shift in range(1, 4):
@@ -103,15 +120,16 @@
     def _():
         pl.semaphore_signal(barrier, inc=1, device_id={"lat": lat + 1}, device_id_type=MESH)
 
-    zero_pad = jnp.zeros((layers + 2, rows, PAD), jnp.float32)
-    for field in (head_x, cond_x):
-        field[:, :, pl.ds(0, PAD)] = zero_pad
-        field[:, :, pl.ds(PAD + width, PAD)] = zero_pad
+    for field, value in ((head_x, 0.0), (cond_x, CLOSED)):
+        filled = jnp.full((layers + 2, rows, PAD), value, jnp.float32)
+        field[:, :, pl.ds(0, PAD)] = filled
+        field[:, :, pl.ds(PAD + width, PAD)] = filled
 
     for side, present in ((0, has_up), (1, has_down)):
         @pl.when(jnp.logical_not(present))
         def _():
-            lrecv[side] = jnp.zeros(lrecv.shape[1:], jnp.float32)
+            lrecv[side, 0] = jnp.zeros(lrecv.shape[2:], jnp.float32)
+            lrecv[side, 1] = jnp.full(lrecv.shape[2:], CLOSED, jnp.float32)
             srecv[side] = jnp.zeros(srecv.shape[1:], jnp.float32)
 
     pl.semaphore_wait(barrier, 3 + jnp.where(has_up, 1, 0) + jnp.where(has_down, 1, 0))
@@ -138,33 +156,41 @@
             device_id_type=MESH,
         )
 
-    for copy in row_loads:
-        copy.wait()
-
-    def boundary(index, carry):
-        cols = pl.ds(pl.multiple_of(index * chunk, 128), chunk)
+    cond_l = lane_table(cond_t, 2.0)
+    shape_l = lane_table(shape_t, 1.0)
+    pore_l = lane_table(pore_t, 1.0)
+
+    def states(part, carry):
+        for copy in loads(part):
+            copy.wait()
+        cols = pl.ds(pl.multiple_of(part * chunk, 128), chunk)
+        wide = pl.ds(pl.multiple_of(part * chunk + PAD, 128), chunk)
+
+        def state(layer, passed):
+            kinds = soil_v[layer, :, cols]
+            steep, pore = lookup(kinds, shape_l), lookup(kinds, pore_l)
+            now = head_x[layer + 1, :, wide]
+            old = old_v[layer, :, cols]
+            wet = jnp.exp(steep * jnp.minimum(now, 0.0))
+            wet_old = jnp.exp(steep * jnp.minimum(old, 0.0))
+            inverse = recip(lookup(kinds, cond_l) * wet)
+            cond_x[layer + 1, :, wide] = inverse
+            for side, row in ((0, 0), (1, rows - 1)):
+                bsend[side, 0, pl.ds(layer, 1), cols] = now[row:row + 1]
+                bsend[side, 1, pl.ds(layer, 1), cols] = inverse[row:row + 1]
+            change = pore * (wet - wet_old) + SPECIFIC_STORAGE * (now - old)
+            base_v[layer, :, cols] = change * (1.0 / TIME_STEP)
+            capd_v[layer, :, cols] = (SPECIFIC_STORAGE + pore * steep * wet) * (1.0 / TIME_STEP)
+            return passed
+
+        lax.fori_loop(0, layers, state, 0, unroll=4)
         for side, present in ((0, has_up), (1, has_down)):
-            saturated, steep = lookup(bsoil[side, :, cols], (cond_t, shape_t))
-            bsend[side, 1, :, cols] = saturated * jnp.exp(steep * jnp.minimum(bsend[side, 0, :, cols], 0.0))
-
             @pl.when(present)
             def _():
-                lat_copy(side, index).start()
+                lat_copy(side, part).start()
         return carry
 
-    lax.fori_loop(0, count, boundary, 0)
-
-    for copy in loads:
-        copy.wait()
-
-    def end_layer(layer):
-        def step(index, carry):
-            cols = pl.ds(pl.multiple_of(index * chunk, 128), chunk)
-            wide = pl.ds(pl.multiple_of(index * chunk + PAD, 128), chunk)
-            saturated, steep = lookup(soil_v[layer, :, cols], (cond_t, shape_t))
-            cond_x[layer + 1, :, wide] = saturated * jnp.exp(steep * jnp.minimum(head_x[layer + 1, :, wide], 0.0))
-            return carry
-        lax.fori_loop(0, count, step, 0)
+    lax.fori_loop(0, count, states, 0)
 
     def m1_copy(place, target):
         slot = jnp.where(top_half, layers + 1, 0) if place == 0 else jnp.where(top_half, 0, layers + 1)
@@ -198,10 +224,8 @@
 
     @pl.when(inner)
     def _():
-        end_layer(layer_at(layers - 1))
         for copy in m1_copy(1, middle):
             copy.start()
-        end_layer(layer_at(0))
         for copy in m1_copy(0, partner):
             copy.start()
 
@@ -217,36 +241,11 @@
 
     @pl.when(is_top)
     def _():
-        end_layer(0)
         wet = ponded[...].astype(jnp.float32) * pond[...]
-        top_v[...] = cond_x[1, :, body] * (2.0 * (wet - head_x[1, :, body]) + 1.0)
+        top_v[...] = 0.5 * recip(cond_x[1, :, body]) * (2.0 * (wet - head_x[1, :, body]) + 1.0)
         for target in range(1, 4):
             x_copy(target).start()
         xrecv[...] = top_v[:, pl.ds(0, window)]
-
-    def state(index, carry):
-        layer = index // count
-        begin = lax.rem(index, count) * chunk
-        cols = pl.ds(pl.multiple_of(begin, 128), chunk)
-        wide = pl.ds(pl.multiple_of(begin + PAD, 128), chunk)
-        saturated, steep, pore = lookup(soil_v[layer, :, cols], (cond_t, shape_t, pore_t))
-        now = head_x[layer + 1, :, wide]
-        old = old_v[layer, :, cols]
-        wet = jnp.exp(steep * jnp.minimum(now, 0.0))
-        wet_old = jnp.exp(steep * jnp.minimum(old, 0.0))
-        value = saturated * wet
-
-        already = (inner & ((layer == 0) | (layer == layers - 1))) | (is_top & (layer == 0))
-
-        @pl.when(jnp.logical_not(already))
-        def _():
-            cond_x[layer + 1, :, wide] = value
-
-        base_v[layer, :, cols] = (pore * (wet - wet_old) + SPECIFIC_STORAGE * (now - old)) * (1.0 / TIME_STEP)
-        capd_v[layer, :, cols] = (SPECIFIC_STORAGE + pore * steep * wet) * (1.0 / TIME_STEP)
-        return carry
-
-    lax.fori_loop(0, layers * count, state, 0)
 
     @pl.when(jnp.logical_not(is_top))
     def _():
@@ -356,35 +355,65 @@
             device_id={"depth": partner}, device_id_type=MESH,
         )
 
-    def out_copy(index):
-        cols = pl.ds(pl.multiple_of(index * chunk, 128), chunk)
-        return pltpu.make_async_copy(out_v.at[:, :, cols], out.at[:, :, cols], out_sem.at[index])
-
     for copy in m1_arrival():
         copy.wait_recv()
 
     row8 = lax.broadcasted_iota(jnp.int32, (rows, chunk), 0)
 
-    def eliminate(index):
+    def local_terms(index, outside):
         cols = pl.ds(pl.multiple_of(index * chunk, 128), chunk)
         mid = pl.ds(pl.multiple_of(index * chunk + PAD, 128), chunk)
         wide = pl.ds(pl.multiple_of(index * chunk, 128), chunk + 2 * PAD)
+        first_cond = 0.5 * recip(cond_x[layer_at(0) + 1, :, mid])
+        wet = ponded[:, cols].astype(jnp.float32) * pond[:, cols]
+        top = first_cond * (2.0 * (wet - head_x[layer_at(0) + 1, :, mid]) + 1.0)
+        face_0 = jnp.where(is_top, 2.0 * first_cond, 0.0)
+        flux_0 = jnp.where(is_top, top, jnp.where(depth == 3, -first_cond, 0.0))
+        size = chunk + 2 * PAD
+        most = chunk + PAD
+
+        def step(place, carry):
+            face_b, flux_b = carry
+            layer = layer_at(place)
+            slot = layer + 1
+            cond_w = cond_x[slot, :, wide]
+            head_w = head_x[slot, :, wide]
+            cond = cond_w[:, PAD:PAD + chunk]
+            here = head_w[:, PAD:PAD + chunk]
+            face = series(cond, cond_x[slot + stride, :, mid])
+            flux = face * (here - head_x[slot + stride, :, mid] + sign)
+            cond_a = pltpu.roll(cond_w, size - 1, 1)[:, :most]
+            head_a = pltpu.roll(head_w, size - 1, 1)[:, :most]
+            along = series(cond_w[:, :most], cond_a) * (head_a - head_w[:, :most])
+            lateral = along[:, PAD:] - pltpu.roll(along, 1, 1)[:, PAD:]
+            across = series(cond, pltpu.roll(cond, rows - 1, 0)) * (pltpu.roll(here, rows - 1, 0) - here)
+            across = jnp.where(row8 == rows - 1, 0.0, across)
+            lateral = lateral + across - pltpu.roll(across, 1, 0)
+            face_v[place, :, cols] = face
+            sum_v[place, :, cols] = capd_v[layer, :, cols] + face + face_b
+            rhs_v[place, :, cols] = flux_b - flux - base_v[layer, :, cols] + lateral
+            return (face, flux)
+
+        face, flux = lax.fori_loop(0, layers, step, (face_0, flux_0), unroll=4)
+        last_v[:, cols] = flux
+        return outside
+
+    lax.fori_loop(0, count, local_terms, 0)
+
+    def eliminate(index):
+        cols = pl.ds(pl.multiple_of(index * chunk, 128), chunk)
         for side, present in ((0, has_up), (1, has_down)):
             @pl.when(present)
             def _():
                 lat_arrival(side, index).wait_recv()
             mine_h, mine_c = bsend[side, 0, :, cols], bsend[side, 1, :, cols]
             theirs_h, theirs_c = lrecv[side, 0, :, cols], lrecv[side, 1, :, cols]
-            flux_v[side] = harmonic(mine_c, theirs_c) * (theirs_h - mine_h)
+            flux_v[side] = series(mine_c, theirs_c) * (theirs_h - mine_h)
 
         @pl.when(outer)
         def _():
-            layer = layer_at(0) + 1
-            first = cond_x[layer, :, mid]
-            wet = ponded[:, cols].astype(jnp.float32) * pond[:, cols]
-            inflow = first * (2.0 * (wet - head_x[layer, :, mid]) + 1.0)
-            m2recv[0, :, cols] = jnp.where(is_top, 2.0 * first, 0.0)
-            m2recv[1, :, cols] = jnp.where(is_top, inflow, -first)
+            m2recv[0, :, cols] = jnp.zeros((rows, chunk), jnp.float32)
+            m2recv[1, :, cols] = jnp.zeros((rows, chunk), jnp.float32)
 
         @pl.when(inner)
         def _():
@@ -393,34 +422,23 @@
         def step(place, carry):
             extra, inflow = carry
             layer = layer_at(place)
-            slot = layer + 1
-            cond_w = cond_x[slot, :, wide]
-            head_w = head_x[slot, :, wide]
-            cond = cond_w[:, PAD:PAD + chunk]
-            here = head_w[:, PAD:PAD + chunk]
-            face = harmonic(cond, cond_x[slot + stride, :, mid])
-            flux = face * (here - head_x[slot + stride, :, mid] + sign)
-            size = chunk + 2 * PAD
-            cond_a = pltpu.roll(cond_w, size - 1, 1)[:, :chunk + PAD]
-            head_a = pltpu.roll(head_w, size - 1, 1)[:, :chunk + PAD]
-            along = harmonic(cond_w[:, :chunk + PAD], cond_a) * (head_a - head_w[:, :chunk + PAD])
-            lateral = along[:, PAD:] - pltpu.roll(along, 1, 1)[:, PAD:]
-            across = harmonic(cond, pltpu.roll(cond, rows - 1, 0)) * (pltpu.roll(here, rows - 1, 0) - here)
-            across = jnp.where(row8 == rows - 1, 0.0, across)
-            lateral = lateral + across - pltpu.roll(across, 1, 0)
             above = flux_v[0, pl.ds(layer, 1), :]
             below = flux_v[1, pl.ds(layer, 1), :]
-            lateral = lateral + jnp.where(row8 == 0, above, jnp.where(row8 == rows - 1, below, 0.0))
-            scale = recip(capd_v[layer, :, cols] + face + extra)
+            lateral = jnp.where(row8 == 0, above, jnp.where(row8 == rows - 1, below, 0.0))
+            face = face_v[place, :, cols]
+            scale = recip(sum_v[place, :, cols] + extra)
             ratio = face * scale
-            value = (inflow - flux - base_v[layer, :, cols] + lateral) * scale
+            value = (inflow + (rhs_v[place, :, cols] + lateral)) * scale
             y_v[place, :, cols] = value
             r_v[place, :, cols] = ratio
-            return (face - face * ratio, flux + face * value)
-
-        extra, inflow = lax.fori_loop(0, layers, step, (m2recv[0, :, cols], m2recv[1, :, cols]))
-        nsend[0, :, cols] = jnp.where(outer, extra, y_v[layers - 1, :, cols])
-        nsend[1, :, cols] = jnp.where(outer, inflow, r_v[layers - 1, :, cols])
+            return (-(face * ratio), face * value)
+
+        extra, inflow = lax.fori_loop(
+            0, layers, step, (m2recv[0, :, cols], m2recv[1, :, cols]), unroll=4
+        )
+        last = layers - 1
+        nsend[0, :, cols] = jnp.where(outer, extra + face_v[last, :, cols], y_v[last, :, cols])
+        nsend[1, :, cols] = jnp.where(outer, inflow + last_v[:, cols], r_v[last, :, cols])
 
         @pl.when(outer)
         def _():
@@ -441,8 +459,7 @@
             out_v[layer, :, cols] = head_x[layer + 1, :, mid] + found
             return found
 
-        found = lax.fori_loop(0, layers, step, beyond)
-        out_copy(index).start()
+        found = lax.fori_loop(0, layers, step, beyond, unroll=4)
         return found
 
     def finish_inner(index):
@@ -463,13 +480,13 @@
         def _():
             eliminate(index)
 
-        @pl.when(index == count)
+        @pl.when(inner & (index >= 1) & (index <= count))
+        def _():
+            finish_inner(index - 1)
+
+        @pl.when(index == count + 1)
         def _():
             surface()
-
-        @pl.when(inner & (index >= 1) & (index <= count))
-        def _():
-            finish_inner(index - 1)
 
         @pl.when(outer & (index >= 2))
         def _():
@@ -494,7 +511,6 @@
             m3_copy(index).wait_send()
             m4_copy(index).wait_send()
 
-        out_copy(index).wait()
         return carry
 
     lax.fori_loop(0, count, drain, 0)
@@ -531,9 +547,9 @@
     dma = pltpu.SemaphoreType.DMA
     return pl.pallas_call(
         functools.partial(kernel, (layers, rows, width, lat_count, chunk)),
-        out_shape=(jax.ShapeDtypeStruct(full, f32), jax.ShapeDtypeStruct((rows, strip), f32)),
+        out_shape=(pltpu.VMEM(full, f32), pltpu.VMEM((rows, strip), f32)),
         in_specs=[any_spec] * 3 + [smem] * 3 + [vmem] * 4,
-        out_specs=(any_spec, vmem),
+        out_specs=(vmem, vmem),
         scratch_shapes=[
             pltpu.VMEM(padded, f32),
             pltpu.VMEM(padded, f32),
@@ -544,8 +560,10 @@
             pltpu.VMEM(full, f32),
             pltpu.VMEM(full, f32),
             pltpu.VMEM(full, f32),
+            pltpu.VMEM(plane, f32),
+            pltpu.VMEM(full, f32),
+            pltpu.VMEM(full, f32),
             pltpu.VMEM((2, 2, layers, width), f32),
-            pltpu.VMEM((2, layers, width), jnp.int32),
             pltpu.VMEM((2, 2, layers, width), f32),
             pltpu.VMEM((2, layers, chunk), f32),
             pltpu.VMEM(pair, f32),
@@ -559,9 +577,7 @@
             pltpu.VMEM((2, 16, window), f32),
             pltpu.VMEM((4, rows + 8, window), f32),
             pltpu.VMEM((rows, window), f32),
-            dma((3,)),
-            dma((2, 2)),
-            dma((count,)),
+            dma((3, count)),
             dma((2, count)),
             dma((2, count)),
             dma((2, 2)),
@@ -577,7 +593,7 @@
             dma((2,)),
         ],
         compiler_params=pltpu.CompilerParams(
-            collective_id=0, has_side_effects=True, vmem_limit_bytes=56 * 1024 * 1024
+            collective_id=0, has_side_effects=True, vmem_limit_bytes=61 * 1024 * 1024
         ),
     )(head, head_old, soil, cond_t, shape_t, pore_t, pond, ground, ponded, river)
 

time: 62 us -> 41.7 us (0.67); the launches traced: 61.9 us -> 40.9 us
  Pallas kernels: 57.5 us -> 38.3 us
  local copies, waits for them, and re-layouts: 3.74 us -> 1.94 us
    pallas_call x1, Pallas kernels: 57.5 us -> 38.3 us  [per_device(): pl.pallas_call(functools.partial(kernel, (layers, rows, width, lat_count,...]
    unnamed x4 -> x2, local copies, waits for them, and re-layouts: 3.74 us -> 1.94 us
where the time goes in v2:
time: 41.7 us; the launch traced here: 40.9 us
  Pallas kernels  38.3 us (92%)
  local copies, waits for them, and re-layouts  1.94 us (5%)
  between operations  0.64 us (2%)
    pallas_call x1, Pallas kernels, per_device(): pl.pallas_call(functools.partial(kernel, (layers, rows, width, lat_count,...  38.3 us
    unnamed x2, local copies, waits for them, and re-layouts  1.94 us

profile of v2, /device:TPU:13, one launch (start us, length us, event | category | flops | bytes accessed | tf_op | source)
XLA Modules:
  0.0 40.9 jit_solution(3874197988892247732)
XLA Ops:
  0.6 38.3 %shard_map.113 = (f32[16,8,4096]{2,1,0:T(8,128)S(1)}, f32[8,1024]{1,0:T(8,128)S(1)}) custom-call(f32[16,8,4096]{2,1,0:T(8,128)} %head.1, f32[16,8,4096]{2,1,0:T(8,128)} %head_old.1, s32[16,8,4096]{2,1,0:T(8,128)} %soil.1, f32[12]{0:T(128)} %cond_t.1, f32[12]{0:T(128)} %shape_t.1, f32[12]{0:T(128)} %pore_t.1, f32[8,4096]{1,0:T(8,128)} %pond.1, ...), custom_call_target="tpu_custom_call" | custom-call | tf_op jit(solution)/shard_map/pallas_call | solution.py:548
  39.0 1.3 %copy.14 = f32[16,8,4096]{2,1,0:T(8,128)} copy(f32[16,8,4096]{2,1,0:T(8,128)S(1)} %get-tuple-element.2) | data formatting | bytes 4194304
  40.3 0.6 %copy.15 = f32[8,1024]{1,0:T(8,128)} copy(f32[8,1024]{1,0:T(8,128)S(1)} %get-tuple-element.3) | data formatting | bytes 65536

commit v3 on v2

--- a/solution.py
+++ b/solution.py
@@ -65,7 +65,7 @@
     head_x, cond_x, old_v, soil_v, base_v, capd_v, face_v, rhs_v, sum_v, last_v, y_v, r_v,
     bsend, lrecv, flux_v, nsend, m2recv, m3recv, m4send, m4recv,
     top_v, xrecv, pack, srecv, sext, lev_v,
-    in_sem, lat_s, lat_r, m1_s, m1_r, n_s, m2_r, m3_r, m4_s, m4_r,
+    in_sem, lat_s, lat_r, ans_s, ans_r, m1_s, m1_r, n_s, m2_r, m3_r, m4_s, m4_r,
     x_s, x_r, surf_s, surf_r,
 ):
     layers, rows, width, lat_count, chunk = sizes
@@ -128,33 +128,51 @@
     for side, present in ((0, has_up), (1, has_down)):
         @pl.when(jnp.logical_not(present))
         def _():
-            lrecv[side, 0] = jnp.zeros(lrecv.shape[2:], jnp.float32)
-            lrecv[side, 1] = jnp.full(lrecv.shape[2:], CLOSED, jnp.float32)
+            flux_v[side] = jnp.zeros(flux_v.shape[1:], jnp.float32)
             srecv[side] = jnp.zeros(srecv.shape[1:], jnp.float32)
 
     pl.semaphore_wait(barrier, 3 + jnp.where(has_up, 1, 0) + jnp.where(has_down, 1, 0))
 
-    def lat_copy(side, index):
+    def neighbour(side):
+        return lat - 1 if side == 0 else lat + 1
+
+    def ask_copy(side, index):
         cols = pl.ds(pl.multiple_of(index * chunk, 128), chunk)
         return pltpu.make_async_remote_copy(
             src_ref=bsend.at[side, :, :, cols],
-            dst_ref=lrecv.at[1 - side, :, :, cols],
-            send_sem=lat_s.at[side, index],
-            recv_sem=lat_r.at[1 - side, index],
-            device_id={"lat": lat - 1 if side == 0 else lat + 1},
+            dst_ref=lrecv.at[:, :, cols],
+            send_sem=lat_s.at[index],
+            recv_sem=lat_r.at[index],
+            device_id={"lat": neighbour(side)},
             device_id_type=MESH,
         )
 
-    def lat_arrival(side, index):
-        cols = pl.ds(pl.multiple_of(index * chunk, 128), chunk)
-        return pltpu.make_async_remote_copy(
-            src_ref=bsend.at[1 - side, :, :, cols],
-            dst_ref=lrecv.at[side, :, :, cols],
-            send_sem=lat_s.at[1 - side, index],
-            recv_sem=lat_r.at[side, index],
-            device_id={"lat": lat - 1 if side == 0 else lat + 1},
+    def answer_copy(side, index):
+        cols = pl.ds(pl.multiple_of(index * chunk, 128), chunk)
+        return pltpu.make_async_remote_copy(
+            src_ref=flux_v.at[side, :, cols],
+            dst_ref=flux_v.at[1 - side, :, cols],
+            send_sem=ans_s.at[index],
+            recv_sem=ans_r.at[index],
+            device_id={"lat": neighbour(side)},
             device_id_type=MESH,
         )
+
+    def answer_arrival(side, index):
+        cols = pl.ds(pl.multiple_of(index * chunk, 128), chunk)
+        return pltpu.make_async_remote_copy(
+            src_ref=flux_v.at[1 - side, :, cols],
+            dst_ref=flux_v.at[side, :, cols],
+            send_sem=ans_s.at[index],
+            recv_sem=ans_r.at[index],
+            device_id={"lat": neighbour(side)},
+            device_id_type=MESH,
+        )
+
+    def by_parity(index):
+        odd = lax.rem(index, 2) == 1
+        even = jnp.logical_not(odd)
+        return ((1, 0, even & has_down, even & has_up), (0, 1, odd & has_up, odd & has_down))
 
     cond_l = lane_table(cond_t, 2.0)
     shape_l = lane_table(shape_t, 1.0)
@@ -184,10 +202,10 @@
             return passed
 
         lax.fori_loop(0, layers, state, 0, unroll=4)
-        for side, present in ((0, has_up), (1, has_down)):
-            @pl.when(present)
+        for side, _, asks, _ in by_parity(part):
+            @pl.when(asks)
             def _():
-                lat_copy(side, part).start()
+                ask_copy(side, part).start()
         return carry
 
     lax.fori_loop(0, count, states, 0)
@@ -400,15 +418,26 @@
 
     lax.fori_loop(0, count, local_terms, 0)
 
+    def answer(index):
+        cols = pl.ds(pl.multiple_of(index * chunk, 128), chunk)
+        for _, side, _, answers in by_parity(index):
+            @pl.when(answers)
+            def _():
+                ask_copy(1 - side, index).wait_recv()
+                mine_h, mine_c = bsend[side, 0, :, cols], bsend[side, 1, :, cols]
+                theirs_h, theirs_c = lrecv[0, :, cols], lrecv[1, :, cols]
+                flux_v[side, :, cols] = series(mine_c, theirs_c) * (theirs_h - mine_h)
+                answer_copy(side, index).start()
+
     def eliminate(index):
         cols = pl.ds(pl.multiple_of(index * chunk, 128), chunk)
-        for side, present in ((0, has_up), (1, has_down)):
-            @pl.when(present)
+        for side, _, asks, _ in by_parity(index):
+            @pl.when(asks)
             def _():
-                lat_arrival(side, index).wait_recv()
-            mine_h, mine_c = bsend[side, 0, :, cols], bsend[side, 1, :, cols]
-            theirs_h, theirs_c = lrecv[side, 0, :, cols], lrecv[side, 1, :, cols]
-            flux_v[side] = series(mine_c, theirs_c) * (theirs_h - mine_h)
+                answer_arrival(side, index).wait_recv()
+        turned = (1 - 2 * lax.rem(index, 2)).astype(jnp.float32)
+        from_above = jnp.where(row8 == 0, turned, 0.0)
+        from_below = jnp.where(row8 == rows - 1, -turned, 0.0)
 
         @pl.when(outer)
         def _():
@@ -422,9 +451,9 @@
         def step(place, carry):
             extra, inflow = carry
             layer = layer_at(place)
-            above = flux_v[0, pl.ds(layer, 1), :]
-            below = flux_v[1, pl.ds(layer, 1), :]
-            lateral = jnp.where(row8 == 0, above, jnp.where(row8 == rows - 1, below, 0.0))
+            above = flux_v[0, pl.ds(layer, 1), cols]
+            below = flux_v[1, pl.ds(layer, 1), cols]
+            lateral = from_above * above + from_below * below
             face = face_v[place, :, cols]
             scale = recip(sum_v[place, :, cols] + extra)
             ratio = face * scale
@@ -478,29 +507,37 @@
     def turn(index, carry):
         @pl.when(index < count)
         def _():
-            eliminate(index)
-
-        @pl.when(inner & (index >= 1) & (index <= count))
-        def _():
-            finish_inner(index - 1)
-
-        @pl.when(index == count + 1)
+            answer(index)
+
+        @pl.when((index >= 1) & (index <= count))
+        def _():
+            eliminate(index - 1)
+
+        @pl.when(inner & (index >= 2) & (index <= count + 1))
+        def _():
+            finish_inner(index - 2)
+
+        @pl.when(index == count + 2)
         def _():
             surface()
 
-        @pl.when(outer & (index >= 2))
-        def _():
-            finish_outer(index - 2)
+        @pl.when(outer & (index >= 3))
+        def _():
+            finish_outer(index - 3)
 
         return carry
 
-    lax.fori_loop(0, count + 2, turn, 0)
+    lax.fori_loop(0, count + 3, turn, 0)
 
     def drain(index, carry):
-        for side, present in ((0, has_up), (1, has_down)):
-            @pl.when(present)
+        for side, other, asks, answers in by_parity(index):
+            @pl.when(asks)
             def _():
-                lat_copy(side, index).wait_send()
+                ask_copy(side, index).wait_send()
+
+            @pl.when(answers)
+            def _():
+                answer_copy(other, index).wait_send()
 
         @pl.when(outer)
         def _():
@@ -564,8 +601,8 @@
             pltpu.VMEM(full, f32),
             pltpu.VMEM(full, f32),
             pltpu.VMEM((2, 2, layers, width), f32),
-            pltpu.VMEM((2, 2, layers, width), f32),
-            pltpu.VMEM((2, layers, chunk), f32),
+            pltpu.VMEM((2, layers, width), f32),
+            pltpu.VMEM((2, layers, width), f32),
             pltpu.VMEM(pair, f32),
             pltpu.VMEM(pair, f32),
             pltpu.VMEM(pair, f32),
@@ -578,8 +615,10 @@
             pltpu.VMEM((4, rows + 8, window), f32),
             pltpu.VMEM((rows, window), f32),
             dma((3, count)),
-            dma((2, count)),
-            dma((2, count)),
+            dma((count,)),
+            dma((count,)),
+            dma((count,)),
+            dma((count,)),
             dma((2, 2)),
             dma((2,)),
             dma((count,)),

time: 41.7 us -> 47.8 us (1.15)
  Pallas kernels: 38.3 us -> 44.8 us
    pallas_call x1, Pallas kernels: 38.3 us -> 44.8 us  [per_device(): pl.pallas_call(functools.partial(kernel, (layers, rows, width, lat_count,...]
where the time goes in v3:
time: 47.8 us; the launch traced here: 47.4 us
  Pallas kernels  44.8 us (94%)
  local copies, waits for them, and re-layouts  1.94 us (4%)
  between operations  0.64 us (1%)
    pallas_call x1, Pallas kernels, per_device(): pl.pallas_call(functools.partial(kernel, (layers, rows, width, lat_count,...  44.8 us
    unnamed x2, local copies, waits for them, and re-layouts  1.94 us

profile of v3, /device:TPU:13, one launch (start us, length us, event | category | flops | bytes accessed | tf_op | source)
XLA Modules:
  0.0 47.4 jit_solution(13173432667298441171)
XLA Ops:
  0.6 44.8 %shard_map.113 = (f32[16,8,4096]{2,1,0:T(8,128)S(1)}, f32[8,1024]{1,0:T(8,128)S(1)}) custom-call(f32[16,8,4096]{2,1,0:T(8,128)} %head.1, f32[16,8,4096]{2,1,0:T(8,128)} %head_old.1, s32[16,8,4096]{2,1,0:T(8,128)} %soil.1, f32[12]{0:T(128)} %cond_t.1, f32[12]{0:T(128)} %shape_t.1, f32[12]{0:T(128)} %pore_t.1, f32[8,4096]{1,0:T(8,128)} %pond.1, ...), custom_call_target="tpu_custom_call" | custom-call | tf_op jit(solution)/shard_map/pallas_call | solution.py:585
  45.5 1.3 %copy.14 = f32[16,8,4096]{2,1,0:T(8,128)} copy(f32[16,8,4096]{2,1,0:T(8,128)S(1)} %get-tuple-element.2) | data formatting | bytes 4194304
  46.8 0.6 %copy.15 = f32[8,1024]{1,0:T(8,128)} copy(f32[8,1024]{1,0:T(8,128)S(1)} %get-tuple-element.3) | data formatting | bytes 65536

commit v4 on v2

--- a/solution.py
+++ b/solution.py
@@ -475,26 +475,28 @@
         m4_copy(index).wait_recv()
         substitute(index, m4recv[:, cols])
 
+    lag = 5
+
     def turn(index, carry):
         @pl.when(index < count)
         def _():
             eliminate(index)
 
-        @pl.when(inner & (index >= 1) & (index <= count))
-        def _():
-            finish_inner(index - 1)
-
-        @pl.when(index == count + 1)
+        @pl.when(inner & (index >= 2) & (index < count + 2))
+        def _():
+            finish_inner(index - 2)
+
+        @pl.when(index == jnp.where(outer, count, count + 2))
         def _():
             surface()
 
-        @pl.when(outer & (index >= 2))
-        def _():
-            finish_outer(index - 2)
+        @pl.when(outer & (index >= lag))
+        def _():
+            finish_outer(index - lag)
 
         return carry
 
-    lax.fori_loop(0, count + 2, turn, 0)
+    lax.fori_loop(0, count + lag, turn, 0)
 
     def drain(index, carry):
         for side, present in ((0, has_up), (1, has_down)):

time: 41.7 us -> 39.1 us (0.938); the launches traced: 40.9 us -> 38.9 us
  Pallas kernels: 38.3 us -> 36.3 us
    pallas_call x1, Pallas kernels: 38.3 us -> 36.3 us  [per_device(): pl.pallas_call(functools.partial(kernel, (layers, rows, width, lat_count,...]
where the time goes in v4:
time: 39.1 us; the launch traced here: 38.9 us
  Pallas kernels  36.3 us (93%)
  local copies, waits for them, and re-layouts  1.94 us (5%)
  between operations  0.64 us (2%)
    pallas_call x1, Pallas kernels, per_device(): pl.pallas_call(functools.partial(kernel, (layers, rows, width, lat_count,...  36.3 us
    unnamed x2, local copies, waits for them, and re-layouts  1.94 us

profile of v4, /device:TPU:13, one launch (start us, length us, event | category | flops | bytes accessed | tf_op | source)
XLA Modules:
  0.0 38.9 jit_solution(16617450087606068268)
XLA Ops:
  0.6 36.3 %shard_map.113 = (f32[16,8,4096]{2,1,0:T(8,128)S(1)}, f32[8,1024]{1,0:T(8,128)S(1)}) custom-call(f32[16,8,4096]{2,1,0:T(8,128)} %head.1, f32[16,8,4096]{2,1,0:T(8,128)} %head_old.1, s32[16,8,4096]{2,1,0:T(8,128)} %soil.1, f32[12]{0:T(128)} %cond_t.1, f32[12]{0:T(128)} %shape_t.1, f32[12]{0:T(128)} %pore_t.1, f32[8,4096]{1,0:T(8,128)} %pond.1, ...), custom_call_target="tpu_custom_call" | custom-call | tf_op jit(solution)/shard_map/pallas_call | solution.py:550
  37.0 1.3 %copy.14 = f32[16,8,4096]{2,1,0:T(8,128)} copy(f32[16,8,4096]{2,1,0:T(8,128)S(1)} %get-tuple-element.2) | data formatting | bytes 4194304
  38.3 0.6 %copy.15 = f32[8,1024]{1,0:T(8,128)} copy(f32[8,1024]{1,0:T(8,128)S(1)} %get-tuple-element.3) | data formatting | bytes 65536

commit v5 on v4

--- a/solution.py
+++ b/solution.py
@@ -160,6 +160,41 @@
     shape_l = lane_table(shape_t, 1.0)
     pore_l = lane_table(pore_t, 1.0)
 
+    def m1_copies(place, target, part):
+        slot = jnp.where(top_half, layers + 1, 0) if place == 0 else jnp.where(top_half, 0, layers + 1)
+        layer = layer_at(0 if place == 0 else layers - 1) + 1
+        wide = pl.ds(pl.multiple_of(part * chunk + PAD, 128), chunk)
+        return [
+            pltpu.make_async_remote_copy(
+                src_ref=field.at[layer, :, wide],
+                dst_ref=field.at[slot, :, wide],
+                send_sem=m1_s.at[place, which, part],
+                recv_sem=m1_r.at[which, part],
+                device_id={"depth": target},
+                device_id_type=MESH,
+            )
+            for which, field in enumerate((head_x, cond_x))
+        ]
+
+    def m1_sends(part):
+        return m1_copies(1, middle, part) + m1_copies(0, partner, part)
+
+    def m1_arrivals(part):
+        slot = jnp.where(top_half, layers + 1, 0)
+        layer = layer_at(layers - 1) + 1
+        wide = pl.ds(pl.multiple_of(part * chunk + PAD, 128), chunk)
+        return [
+            pltpu.make_async_remote_copy(
+                src_ref=field.at[layer, :, wide],
+                dst_ref=field.at[slot, :, wide],
+                send_sem=m1_s.at[1, which, part],
+                recv_sem=m1_r.at[which, part],
+                device_id={"depth": partner},
+                device_id_type=MESH,
+            )
+            for which, field in enumerate((head_x, cond_x))
+        ]
+
     def states(part, carry):
         for copy in loads(part):
             copy.wait()
@@ -188,46 +223,14 @@
             @pl.when(present)
             def _():
                 lat_copy(side, part).start()
+
+        @pl.when(inner)
+        def _():
+            for copy in m1_sends(part):
+                copy.start()
         return carry
 
     lax.fori_loop(0, count, states, 0)
-
-    def m1_copy(place, target):
-        slot = jnp.where(top_half, layers + 1, 0) if place == 0 else jnp.where(top_half, 0, layers + 1)
-        layer = layer_at(0 if place == 0 else layers - 1) + 1
-        return [
-            pltpu.make_async_remote_copy(
-                src_ref=field.at[layer, :, body],
-                dst_ref=field.at[slot, :, body],
-                send_sem=m1_s.at[place, which],
-                recv_sem=m1_r.at[which],
-                device_id={"depth": target},
-                device_id_type=MESH,
-            )
-            for which, field in enumerate((head_x, cond_x))
-        ]
-
-    def m1_arrival():
-        slot = jnp.where(top_half, layers + 1, 0)
-        layer = layer_at(layers - 1) + 1
-        return [
-            pltpu.make_async_remote_copy(
-                src_ref=field.at[layer, :, body],
-                dst_ref=field.at[slot, :, body],
-                send_sem=m1_s.at[1, which],
-                recv_sem=m1_r.at[which],
-                device_id={"depth": partner},
-                device_id_type=MESH,
-            )
-            for which, field in enumerate((head_x, cond_x))
-        ]
-
-    @pl.when(inner)
-    def _():
-        for copy in m1_copy(1, middle):
-            copy.start()
-        for copy in m1_copy(0, partner):
-            copy.start()
 
     def x_copy(target):
         return pltpu.make_async_remote_copy(
@@ -246,6 +249,74 @@
         for target in range(1, 4):
             x_copy(target).start()
         xrecv[...] = top_v[:, pl.ds(0, window)]
+
+    def m2_copy(index):
+        cols = pl.ds(pl.multiple_of(index * chunk, 128), chunk)
+        return pltpu.make_async_remote_copy(
+            src_ref=nsend.at[:, :, cols], dst_ref=m2recv.at[:, :, cols],
+            send_sem=n_s.at[index], recv_sem=m2_r.at[index],
+            device_id={"depth": partner}, device_id_type=MESH,
+        )
+
+    def m3_copy(index):
+        cols = pl.ds(pl.multiple_of(index * chunk, 128), chunk)
+        return pltpu.make_async_remote_copy(
+            src_ref=nsend.at[:, :, cols], dst_ref=m3recv.at[:, :, cols],
+            send_sem=n_s.at[index], recv_sem=m3_r.at[index],
+            device_id={"depth": middle}, device_id_type=MESH,
+        )
+
+    def m4_copy(index):
+        cols = pl.ds(pl.multiple_of(index * chunk, 128), chunk)
+        return pltpu.make_async_remote_copy(
+            src_ref=m4send.at[:, cols], dst_ref=m4recv.at[:, cols],
+            send_sem=m4_s.at[index], recv_sem=m4_r.at[index],
+            device_id={"depth": partner}, device_id_type=MESH,
+        )
+
+    row8 = lax.broadcasted_iota(jnp.int32, (rows, chunk), 0)
+
+    def local_terms(index, outside):
+        for copy in m1_arrivals(index):
+            copy.wait_recv()
+        cols = pl.ds(pl.multiple_of(index * chunk, 128), chunk)
+        mid = pl.ds(pl.multiple_of(index * chunk + PAD, 128), chunk)
+        wide = pl.ds(pl.multiple_of(index * chunk, 128), chunk + 2 * PAD)
+        first_cond = 0.5 * recip(cond_x[layer_at(0) + 1, :, mid])
+        wet = ponded[:, cols].astype(jnp.float32) * pond[:, cols]
+        top = first_cond * (2.0 * (wet - head_x[layer_at(0) + 1, :, mid]) + 1.0)
+        face_0 = jnp.where(is_top, 2.0 * first_cond, 0.0)
+        flux_0 = jnp.where(is_top, top, jnp.where(depth == 3, -first_cond, 0.0))
+        size = chunk + 2 * PAD
+        most = chunk + PAD
+
+        def step(place, carry):
+            face_b, flux_b = carry
+            layer = layer_at(place)
+            slot = layer + 1
+            cond_w = cond_x[slot, :, wide]
+            head_w = head_x[slot, :, wide]
+            cond = cond_w[:, PAD:PAD + chunk]
+            here = head_w[:, PAD:PAD + chunk]
+            face = series(cond, cond_x[slot + stride, :, mid])
+            flux = face * (here - head_x[slot + stride, :, mid] + sign)
+            cond_a = pltpu.roll(cond_w, size - 1, 1)[:, :most]
+            head_a = pltpu.roll(head_w, size - 1, 1)[:, :most]
+            along = series(cond_w[:, :most], cond_a) * (head_a - head_w[:, :most])
+            lateral = along[:, PAD:] - pltpu.roll(along, 1, 1)[:, PAD:]
+            across = series(cond, pltpu.roll(cond, rows - 1, 0)) * (pltpu.roll(here, rows - 1, 0) - here)
+            across = jnp.where(row8 == rows - 1, 0.0, across)
+            lateral = lateral + across - pltpu.roll(across, 1, 0)
+            face_v[place, :, cols] = face
+            sum_v[place, :, cols] = capd_v[layer, :, cols] + face + face_b
+            rhs_v[place, :, cols] = flux_b - flux - base_v[layer, :, cols] + lateral
+            return (face, flux)
+
+        face, flux = lax.fori_loop(0, layers, step, (face_0, flux_0), unroll=4)
+        last_v[:, cols] = flux
+        return outside
+
+    lax.fori_loop(0, count, local_terms, 0)
 
     @pl.when(jnp.logical_not(is_top))
     def _():
@@ -331,75 +402,6 @@
         offset = pl.multiple_of(depth * strip - begin, 128)
         surf[...] = lev_v[:, pl.ds(offset, strip)]
 
-    def m2_copy(index):
-        cols = pl.ds(pl.multiple_of(index * chunk, 128), chunk)
-        return pltpu.make_async_remote_copy(
-            src_ref=nsend.at[:, :, cols], dst_ref=m2recv.at[:, :, cols],
-            send_sem=n_s.at[index], recv_sem=m2_r.at[index],
-            device_id={"depth": partner}, device_id_type=MESH,
-        )
-
-    def m3_copy(index):
-        cols = pl.ds(pl.multiple_of(index * chunk, 128), chunk)
-        return pltpu.make_async_remote_copy(
-            src_ref=nsend.at[:, :, cols], dst_ref=m3recv.at[:, :, cols],
-            send_sem=n_s.at[index], recv_sem=m3_r.at[index],
-            device_id={"depth": middle}, device_id_type=MESH,
-        )
-
-    def m4_copy(index):
-        cols = pl.ds(pl.multiple_of(index * chunk, 128), chunk)
-        return pltpu.make_async_remote_copy(
-            src_ref=m4send.at[:, cols], dst_ref=m4recv.at[:, cols],
-            send_sem=m4_s.at[index], recv_sem=m4_r.at[index],
-            device_id={"depth": partner}, device_id_type=MESH,
-        )
-
-    for copy in m1_arrival():
-        copy.wait_recv()
-
-    row8 = lax.broadcasted_iota(jnp.int32, (rows, chunk), 0)
-
-    def local_terms(index, outside):
-        cols = pl.ds(pl.multiple_of(index * chunk, 128), chunk)
-        mid = pl.ds(pl.multiple_of(index * chunk + PAD, 128), chunk)
-        wide = pl.ds(pl.multiple_of(index * chunk, 128), chunk + 2 * PAD)
-        first_cond = 0.5 * recip(cond_x[layer_at(0) + 1, :, mid])
-        wet = ponded[:, cols].astype(jnp.float32) * pond[:, cols]
-        top = first_cond * (2.0 * (wet - head_x[layer_at(0) + 1, :, mid]) + 1.0)
-        face_0 = jnp.where(is_top, 2.0 * first_cond, 0.0)
-        flux_0 = jnp.where(is_top, top, jnp.where(depth == 3, -first_cond, 0.0))
-        size = chunk + 2 * PAD
-        most = chunk + PAD
-
-        def step(place, carry):
-            face_b, flux_b = carry
-            layer = layer_at(place)
-            slot = layer + 1
-            cond_w = cond_x[slot, :, wide]
-            head_w = head_x[slot, :, wide]
-            cond = cond_w[:, PAD:PAD + chunk]
-            here = head_w[:, PAD:PAD + chunk]
-            face = series(cond, cond_x[slot + stride, :, mid])
-            flux = face * (here - head_x[slot + stride, :, mid] + sign)
-            cond_a = pltpu.roll(cond_w, size - 1, 1)[:, :most]
-            head_a = pltpu.roll(head_w, size - 1, 1)[:, :most]
-            along = series(cond_w[:, :most], cond_a) * (head_a - head_w[:, :most])
-            lateral = along[:, PAD:] - pltpu.roll(along, 1, 1)[:, PAD:]
-            across = series(cond, pltpu.roll(cond, rows - 1, 0)) * (pltpu.roll(here, rows - 1, 0) - here)
-            across = jnp.where(row8 == rows - 1, 0.0, across)
-            lateral = lateral + across - pltpu.roll(across, 1, 0)
-            face_v[place, :, cols] = face
-            sum_v[place, :, cols] = capd_v[layer, :, cols] + face + face_b
-            rhs_v[place, :, cols] = flux_b - flux - base_v[layer, :, cols] + lateral
-            return (face, flux)
-
-        face, flux = lax.fori_loop(0, layers, step, (face_0, flux_0), unroll=4)
-        last_v[:, cols] = flux
-        return outside
-
-    lax.fori_loop(0, count, local_terms, 0)
-
     def eliminate(index):
         cols = pl.ds(pl.multiple_of(index * chunk, 128), chunk)
         for side, present in ((0, has_up), (1, has_down)):
@@ -512,6 +514,8 @@
         def _():
             m3_copy(index).wait_send()
             m4_copy(index).wait_send()
+            for copy in m1_sends(index):
+                copy.wait_send()
 
         return carry
 
@@ -520,11 +524,6 @@
         @pl.when(present)
         def _():
             surf_copy(side).wait_send()
-
-    @pl.when(inner)
-    def _():
-        for copy in m1_copy(1, middle) + m1_copy(0, partner):
-            copy.wait_send()
 
     @pl.when(is_top)
     def _():
@@ -582,8 +581,8 @@
             dma((3, count)),
             dma((2, count)),
             dma((2, count)),
-            dma((2, 2)),
-            dma((2,)),
+            dma((2, 2, count)),
+            dma((2, count)),
             dma((count,)),
             dma((count,)),
             dma((count,)),

time: 39.1 us -> 39.5 us (1.010)
  Pallas kernels: 36.3 us -> 36.7 us
    pallas_call x1, Pallas kernels: 36.3 us -> 36.7 us  [per_device(): pl.pallas_call(functools.partial(kernel, (layers, rows, width, lat_count,...]
where the time goes in v5:
time: 39.5 us; the launch traced here: 39.3 us
  Pallas kernels  36.7 us (93%)
  local copies, waits for them, and re-layouts  1.94 us (5%)
  between operations  0.64 us (2%)
    pallas_call x1, Pallas kernels, per_device(): pl.pallas_call(functools.partial(kernel, (layers, rows, width, lat_count,...  36.7 us
    unnamed x2, local copies, waits for them, and re-layouts  1.94 us

profile of v5, /device:TPU:13, one launch (start us, length us, event | category | flops | bytes accessed | tf_op | source)
XLA Modules:
  0.0 39.3 jit_solution(16270960862228636800)
XLA Ops:
  0.6 36.7 %shard_map.113 = (f32[16,8,4096]{2,1,0:T(8,128)S(1)}, f32[8,1024]{1,0:T(8,128)S(1)}) custom-call(f32[16,8,4096]{2,1,0:T(8,128)} %head.1, f32[16,8,4096]{2,1,0:T(8,128)} %head_old.1, s32[16,8,4096]{2,1,0:T(8,128)} %soil.1, f32[12]{0:T(128)} %cond_t.1, f32[12]{0:T(128)} %shape_t.1, f32[12]{0:T(128)} %pore_t.1, f32[8,4096]{1,0:T(8,128)} %pond.1, ...), custom_call_target="tpu_custom_call" | custom-call | tf_op jit(solution)/shard_map/pallas_call | solution.py:549
  37.4 1.3 %copy.14 = f32[16,8,4096]{2,1,0:T(8,128)} copy(f32[16,8,4096]{2,1,0:T(8,128)S(1)} %get-tuple-element.2) | data formatting | bytes 4194304
  38.7 0.6 %copy.15 = f32[8,1024]{1,0:T(8,128)} copy(f32[8,1024]{1,0:T(8,128)S(1)} %get-tuple-element.3) | data formatting | bytes 65536
